TPU v7x, 32 devices: a whole 2x2x4 slice. The times are simulated.
32 devices in a mesh: gz: 8 (over z, y), gy: 4 (over x, core).
Axes of the slice: x: 2, y: 2, z: 4, core: 2. Of those that a mesh axis runs over, the one named last changes fastest.
Arguments:
- patch_force: float32 [4096, 24, 128], P(('gz', 'gy')), may hold values from -36 to 36
- patch_owner: int32 [4096], P(('gz', 'gy')), may hold values from 0 to 31, as said below
- patch_voxel: int32 [4096, 128], P(('gz', 'gy')), may hold values from 0 to 16383
- patch_live: int32 [4096, 8], P(('gz', 'gy')), may hold values from 64 to 128
- voxel_mask: int32 [64, 32, 256], P('gz', 'gy'), may hold values 0 or 1
- element_matrix: float32 [24, 24], replicated, may hold values from -0.2 to 6.5, as said below
Outputs:
- displacement: float32 [24, 64, 32, 256], P(None, 'gz', 'gy')
- residual: float32 [24, 64, 32, 256], P(None, 'gz', 'gy')
Inputs may be any that keep to these rules, and one draw needn't show every extreme that they name: `patch_owner`: within the 128 patch blocks of one device no owner appears more than 8 times, and in every device's blocks some owner appears exactly 8 times. `element_matrix`: symmetric positive definite.
All inputs are finite; a program needn't handle non-finite values. No bound on the sum of `voxel_mask` on one device may be relied on, other than what follows from the above.
Results may differ from a plain program's by a relative error of at most 0.00029.
Values sent between devices are 32-bit elements; how exact they have to be, the bound alone decides.
A program may use at most 128 MiB of HBM per device.

v0:
```python
import jax
import jax.numpy as jnp
from jax import lax
from jax.sharding import PartitionSpec as P

LOADS = 8
ITERS = 2


spring = 0.5
highest = lax.Precision.HIGHEST


def padded_2(block, sides, width):
    for axis, dim in sides:
        count = lax.axis_size(axis)
        forward = [(i, i + 1) for i in range(count - 1)]
        backward = [(target, source) for source, target in forward]
        low = lax.ppermute(
            lax.slice_in_dim(block, block.shape[dim] - width, None, axis=dim), axis, forward
        )
        high = lax.ppermute(lax.slice_in_dim(block, 0, width, axis=dim), axis, backward)
        block = jnp.concatenate([low, block, high], axis=dim)
    return block


def shifted(value, axis, steps):
    count = lax.axis_size(axis)
    leading, last = (max(0, -steps), min(count, count - steps))
    return lax.ppermute(value, axis, [(source, source + steps) for source in range(leading, last)])


def shift_left(values):
    filler = jnp.zeros(values.shape[:-1] + (1,), values.dtype)
    return jnp.concatenate([values[..., 1:], filler], axis=-1)


def shift_right(values):
    filler = jnp.zeros(values.shape[:-1] + (1,), values.dtype)
    return jnp.concatenate([filler, values[..., :-1]], axis=-1)


def plane_terms(padded, modulus, element_matrix, plane_index):
    channels = padded.shape[0]
    load_count = channels // 3
    width_rows = padded.shape[2] - 2
    width_cols = padded.shape[3]
    layer = lax.dynamic_slice_in_dim(padded, plane_index, 2, 1)
    corners = []
    for corner_z in (0, 1):
        for corner_y in (0, 1):
            sliced = layer[:, corner_z, corner_y : corner_y + width_rows + 1, :]
            corners.append(sliced)
            corners.append(shift_left(sliced))
    stacked = jnp.stack(corners, 0).reshape(24, load_count, -1)
    weights = lax.dynamic_index_in_dim(modulus, plane_index, 0, False).reshape(1, 1, -1)
    forces = jnp.einsum("ij,jlq->ilq", element_matrix, stacked, precision=highest) * weights
    forces = forces.reshape(8, channels, width_rows + 1, width_cols)
    lower_part = jnp.zeros((channels, width_rows, width_cols), forces.dtype)
    upper_part = jnp.zeros((channels, width_rows, width_cols), forces.dtype)
    for corner_y in (0, 1):
        start_y = 1 - corner_y
        lower_part = lower_part + forces[corner_y * 2][:, start_y : start_y + width_rows, :]
        lower_part = lower_part + shift_right(
            forces[corner_y * 2 + 1][:, start_y : start_y + width_rows, :]
        )
        upper_part = upper_part + forces[4 + corner_y * 2][:, start_y : start_y + width_rows, :]
        upper_part = upper_part + shift_right(
            forces[5 + corner_y * 2][:, start_y : start_y + width_rows, :]
        )
    return (lower_part, upper_part)


def assemble(padded, modulus, element_matrix):
    plane_count = modulus.shape[0]
    channels = padded.shape[0]
    width_rows = padded.shape[2] - 2
    width_cols = padded.shape[3]
    empty = jnp.zeros((channels, plane_count, width_rows, width_cols), jnp.float32)

    def one_plane(plane_index, buffers):
        lower_buf, upper_buf = buffers
        lower_part, upper_part = plane_terms(padded, modulus, element_matrix, plane_index)
        lower_buf = lax.dynamic_update_slice_in_dim(lower_buf, lower_part[:, None], plane_index, 1)
        upper_buf = lax.dynamic_update_slice_in_dim(upper_buf, upper_part[:, None], plane_index, 1)
        return (lower_buf, upper_buf)

    lower_buf, upper_buf = lax.fori_loop(0, plane_count, one_plane, (empty, empty))
    return lower_buf[:, 1:] + upper_buf[:, :-1]


def apply_operator(vector_field, modulus, element_matrix):
    padded = padded_2(vector_field, (("gz", 1), ("gy", 2)), 1)
    return assemble(padded, modulus, element_matrix) + spring * vector_field


def gram_local(first, second):
    return jnp.einsum(
        "clq,cmq->lm", first.reshape(3, LOADS, -1), second.reshape(3, LOADS, -1), precision=highest
    )


def combine(vector_field, matrix):
    mixed = jnp.einsum("clq,lm->cmq", vector_field.reshape(3, LOADS, -1), matrix, precision=highest)
    return mixed.reshape(vector_field.shape)


def solve_small(matrix, target):
    factor = jnp.linalg.cholesky(matrix)
    halfway = lax.linalg.triangular_solve(factor, target, left_side=True, lower=True)
    return lax.linalg.triangular_solve(
        factor, halfway, left_side=True, lower=True, transpose_a=True
    )


def pair_sums(residual, applied):
    return lax.psum((gram_local(residual, residual), gram_local(residual, applied)), ("gz", "gy"))


def body(patch_force, patch_owner, patch_voxel, patch_live, voxel_mask, element_matrix):
    patch_total = patch_force.shape[0]
    channels = patch_force.shape[1]
    slot_width = patch_force.shape[2]
    slab_depth, slab_rows, slab_cols = voxel_mask.shape
    groups_z = lax.axis_size("gz")
    groups_y = lax.axis_size("gy")
    device_count = groups_z * groups_y
    capacity = max(2, (2 * patch_total + device_count - 1) // device_count)
    load_of = jnp.arange(channels, dtype=jnp.int32) % LOADS
    live_count = patch_live[:, load_of]
    keep = jnp.arange(slot_width, dtype=jnp.int32)[None, None, :] < live_count[:, :, None]
    loaded = jnp.where(keep, patch_force, jnp.zeros_like(patch_force))
    owner_hits = (
        patch_owner[:, None] == jnp.arange(device_count, dtype=jnp.int32)[None, :]
    ).astype(jnp.int32)
    earlier = jnp.cumsum(owner_hits, axis=0) - owner_hits
    rank_within = jnp.sum(earlier * owner_hits, axis=1)
    target_slot = patch_owner * capacity + rank_within
    send_force = (
        jnp.zeros((device_count * capacity, channels, slot_width), jnp.float32)
        .at[target_slot]
        .set(loaded)
    )
    send_ids = (
        jnp.zeros((device_count * capacity, slot_width), jnp.int32).at[target_slot].set(patch_voxel)
    )
    send_force = send_force.reshape(device_count, capacity, channels, slot_width)
    send_ids = send_ids.reshape(device_count, capacity, slot_width)
    got_force, got_ids = (
        lax.all_to_all(send_force, ("gz", "gy"), split_axis=0, concat_axis=0, tiled=True),
        lax.all_to_all(send_ids, ("gz", "gy"), split_axis=0, concat_axis=0, tiled=True),
    )
    got_force = got_force.reshape(-1, channels, slot_width)
    flat_ids = got_ids.reshape(-1)
    contrib = jnp.transpose(got_force, (1, 0, 2)).reshape(channels, -1)
    volume = slab_depth * slab_rows * slab_cols
    nodal_force = jnp.zeros((channels, volume), jnp.float32).at[:, flat_ids].add(contrib)
    nodal_force = nodal_force.reshape(channels, slab_depth, slab_rows, slab_cols)
    top_plane = voxel_mask[-1]
    below_plane = shifted(top_plane, "gz", 1)
    mask_z = jnp.concatenate([below_plane[None], voxel_mask], axis=0)
    last_row = mask_z[:, -1, :]
    beside_row = shifted(last_row, "gy", 1)
    mask_full = jnp.concatenate([beside_row[:, None, :], mask_z], axis=1)
    modulus = mask_full.astype(jnp.float32).reshape(slab_depth + 1, (slab_rows + 1) * slab_cols)
    displacement = jnp.zeros_like(nodal_force)
    residual = nodal_force
    applied = apply_operator(residual, modulus, element_matrix)
    norm_gram, curvature = pair_sums(residual, applied)
    direction = residual
    along = applied
    for iteration in range(ITERS):
        curvature = 0.5 * (curvature + curvature.T)
        step_alpha = solve_small(curvature, norm_gram)
        displacement = displacement + combine(direction, step_alpha)
        residual = residual - combine(along, step_alpha)
        if iteration + 1 < ITERS:
            applied = apply_operator(residual, modulus, element_matrix)
            norm_next, cross_gram = pair_sums(residual, applied)
            step_beta = solve_small(norm_gram, norm_next)
            direction = residual + combine(direction, step_beta)
            along = applied + combine(along, step_beta)
            carried = jnp.dot(
                jnp.dot(step_beta.T, curvature, precision=highest), step_beta, precision=highest
            )
            curvature = cross_gram - carried
            norm_gram = norm_next
    return (displacement, residual)


def solution(mesh):
    placed = (
        P(("gz", "gy"), None, None),
        P(("gz", "gy")),
        P(("gz", "gy"), None),
        P(("gz", "gy"), None),
        P("gz", "gy", None),
        P(),
    )
    return jax.shard_map(
        body,
        mesh=mesh,
        in_specs=placed,
        out_specs=(P(None, "gz", "gy", None), P(None, "gz", "gy", None)),
        check_vma=False,
    )
```

profile of v0, /device:TPU:0, one launch (start us, length us, event | category | flops | bytes accessed | tf_op | source)
XLA Modules:
  0.0 1185.8 jit_solution(16717125036263307700)
XLA Ops:
  4.9 7.3 all-to-all-start
  16.4 15.6 %scatter_fusion = f32[256,24,128]{2,1,0:T(8,128)} fusion(f32[256,24,128]{2,1,0:T(8,128)} %broadcast_in_dim.60, s32[128]{0:T(128)S(1)} %compare_select_fusion.2, f32[128,24,128]{2,1,0:T(8,128)S(1)} %fusion.28), kind=kCustom, calls=%fused_computation.2 | custom fusion | bytes 4719104 | tf_op jit(solution)/shard_map/scatter | solution.py:142
  32.0 6.0 all-to-all-start.1
  38.2 71.3 %all-to-all-done.1 = f32[32,8,24,128]{3,2,1,0:T(8,128)} async-done(((f32[32,8,24,128]{3,2,1,0:T(8,128)}), f32[32,8,24,128]{3,2,1,0:T(8,128)}, u32[]{:S(2)}, u32[]{:S(2)}) %all-to-all-start.1) | async-done | bytes 3145760 | tf_op jit(solution)/shard_map/all_to_all | solution.py:150
  109.5 10.0 copy.213
  119.4 209.4 %scatter_custom_fusion.2 = f32[24,16384]{0,1:T(8,128)} fusion(s32[32768]{0:T(1024)S(1)} %bitcast.323, f32[32768,24]{1,0:T(8,128)} %bitcast.312, f32[]{:T(128)} %constant.138.clone.1), kind=kCustom, calls=%fused_computation.69 | custom fusion | flops 786432 | bytes 1573376 | tf_op jit(solution)/shard_map/scatter-add | solution.py:157
  328.8 5.2 copy.215
  334.1 5.1 collective-permute-start
  340.5 4.5 collective-permute-start.4
  348.8 5.9 collective-permute-start.2
  357.4 6.1 copy.222
  363.5 5.1 copy.214
  368.6 3.5 fusion.29
  372.1 3.7 pad_maximum_fusion
  378.6 334.1 %while.30 = (s32[]{:T(128)}, f32[24,9,8,256]{3,0,2,1:T(8,128)}, f32[24,9,8,256]{3,0,2,1:T(8,128)}, f32[24,10,10,256]{3,2,0,1:T(8,128)}, f32[24,24]{1,0:T(8,128)S...) while((s32[]{:T(128)}, f32[24,9,8,256]{3,0,2,1:T(8,128)}, f32[24,9,8,256]{3,0,2,1:T(8,128)}, ...), condition=%wide.region_6.7_spmd, body=%wide.region_5.6_spmd.sunk | while | flops 128139264 | bytes 31001880 | solution.py:88
  391.2 2.6 reshape.281
  428.3 2.6 reshape.281
  465.4 2.6 reshape.281
  502.6 2.6 reshape.281
  539.7 2.6 reshape.281
  576.8 2.6 reshape.281
  614.0 2.6 reshape.281
  651.1 2.6 reshape.281
  688.2 2.6 reshape.281
  712.8 2.7 multiply_add_fusion.1
  718.8 3.7 fusion.32
  722.5 39.0 %all-reduce.17 = (f32[8,8]{0,1:T(8,128)S(1)}, f32[8,8]{1,0:T(8,128)S(1)}) all-reduce(f32[8,8]{0,1:T(8,128)S(1)} %fusion.29, f32[8,8]{1,0:T(8,128)S(1)} %fusion.32), channel_id=1, replica_groups=mesh['gz'=8,'gy'=4] {'gz','gy'}, use_global_device_ids=true, to_apply=%region_10.12 | all-reduce | flops 128 | bytes 1024 | tf_op jit(solution)/shard_map/psum | solution.py:117
  764.8 2.8 fusion.65
  773.9 4.2 collective-permute-start.6
  781.4 4.4 collective-permute-done.7
  793.1 6.1 convolution_bitcast_fusion.2
  799.1 2.8 pad_maximum_fusion.1
  804.8 301.5 %while.31 = (s32[]{:T(128)}, f32[24,9,8,256]{3,0,2,1:T(8,128)}, f32[24,9,8,256]{3,0,2,1:T(8,128)}, f32[24,10,10,256]{3,0,2,1:T(8,128)}, f32[24,24]{1,0:T(8,128)S...) while((s32[]{:T(128)}, f32[24,9,8,256]{3,0,2,1:T(8,128)}, f32[24,9,8,256]{3,0,2,1:T(8,128)}, ...), condition=%wide.region_12.16_spmd, body=%wide.region_11.15_spmd.sunk | while | flops 128139264 | bytes 32254724 | solution.py:88
  813.9 2.6 reshape.282
  847.4 2.6 reshape.282
  880.9 2.6 reshape.282
  914.4 2.6 reshape.282
  947.8 2.6 reshape.282
  981.3 2.6 reshape.282
  1014.8 2.6 reshape.282
  1048.3 2.6 reshape.282
  1081.8 2.6 reshape.282
  1106.4 2.7 multiply_add_fusion
  1111.9 2.7 reshape.203
  1114.6 4.9 convolution_bitcast_fusion.3
  1119.5 44.0 %all-reduce.16 = (f32[8,8]{1,0:T(8,128)S(1)}, f32[8,8]{1,0:T(8,128)S(1)}) all-reduce(f32[8,8]{1,0:T(8,128)S(1)} %copy-done.14, f32[8,8]{1,0:T(8,128)S(1)} %convolution_bitcast_fusion.3), channel_id=1, replica_groups=mesh['gz'=8,'gy'=4] {'gz','gy'}, use_global_device_ids=true, to_apply=%region_14.18 | all-reduce | flops 128 | bytes 1024 | tf_op jit(solution)/shard_map/psum | solution.py:117
  1163.8 2.9 fusion.52
  1166.9 2.7 fusion.18
  (865 shorter events, 650.7 us)
Async XLA Ops:
  0.6 11.6 copy-start
  4.9 27.2 %all-to-all-start = ((s32[32,8,128]{2,1,0:T(8,128)}), s32[32,8,128]{2,1,0:T(8,128)S(1)}, u32[]{:S(2)}, u32[]{:S(2)}) async-start(s32[32,8,128]{2,1,0:T(8,128)} %bitcast.32), calls=%async_computation | async-start | bytes 262144 | tf_op jit(solution)/shard_map/all_to_all | solution.py:151
  32.0 77.4 %all-to-all-start.1 = ((f32[32,8,24,128]{3,2,1,0:T(8,128)}), f32[32,8,24,128]{3,2,1,0:T(8,128)}, u32[]{:S(2)}, u32[]{:S(2)}) async-start(f32[32,8,24,128]{3,2,1,0:T(8,128)} %bitcast.311), calls=%async_computation.1 | async-start | bytes 6291456 | tf_op jit(solution)/shard_map/all_to_all | solution.py:150
  328.8 11.7 copy-start.13
  334.1 13.7 %collective-permute-start = (f32[24,1,8,256]{3,2,0,1:T(8,128)S(1)}, f32[24,1,8,256]{3,2,0,1:T(8,128)S(1)}, u32[]{:S(2)}, u32[]{:S(2)}) collective-permute-start(f32[24,1,8,256]{3,2,0,1:T(8,128)S(1)} %get-tuple-element.319), channel_id=1, source_target_pairs={{0,4},{4,8},{8,12},{12,16},{16,20},{20,24},{24,28},{1,5},{5,9},{9,... | collective-permute-start | bytes 589832 | tf_op jit(solution)/shard_map/ppermute | solution.py:19
  339.2 8.5 collective-permute-start.1
  340.5 5.9 collective-permute-start.4
  346.4 10.1 collective-permute-start.5
  348.8 23.2 %collective-permute-start.2 = (f32[24,10,1,256]{3,2,0,1:T(1,128)}, f32[24,10,1,256]{3,2,0,1:T(1,128)}, u32[]{:S(2)}, u32[]{:S(2)}) collective-permute-start(f32[24,10,1,256]{3,2,0,1:T(1,128)} %get-tuple-element.315), channel_id=1, source_target_pairs={{0,1},{1,2},{2,3},{4,5},{5,6},{6,7},{8,9},{9,10},{10,11},{12,13},{... | collective-permute-start | bytes 737288 | tf_op jit(solution)/shard_map/ppermute | solution.py:19
  354.8 17.3 %collective-permute-start.3 = (f32[24,10,1,256]{3,2,0,1:T(1,128)}, f32[24,10,1,256]{3,2,0,1:T(1,128)}, u32[]{:S(2)}, u32[]{:S(2)}) collective-permute-start(f32[24,10,1,256]{3,2,0,1:T(1,128)} %get-tuple-element.316), channel_id=1, source_target_pairs={{1,0},{2,1},{3,2},{5,4},{6,5},{7,6},{9,8},{10,9},{11,10},{13,12},{... | collective-permute-start | bytes 737288 | tf_op jit(solution)/shard_map/ppermute | solution.py:22
  375.8 2.9 copy-start.12
  718.8 45.8 %copy-start.6 = (f32[3,8,16384]{2,1,0:T(8,128)}, f32[3,8,16384]{2,1,0:T(8,128)S(1)}, u32[]{:S(2)}) copy-start(f32[3,8,16384]{2,1,0:T(8,128)S(1)} %reshape.201) | copy-start | bytes 4718596
  767.6 4.4 copy-start.4
  771.5 1.4 copy-start.7
  772.9 6.5 copy-start.16
  773.8 25.3 %copy-start.2 = (f32[24,8,8,256]{3,0,2,1:T(8,128)}, f32[24,8,8,256]{3,0,2,1:T(8,128)S(1)}, u32[]{:S(2)}) copy-start(f32[24,8,8,256]{3,0,2,1:T(8,128)S(1)} %copy_subtract_fusion.1) | copy-start | bytes 4718596
  773.9 7.5 collective-permute-start.6
  778.1 7.7 collective-permute-start.7
  786.7 12.4 %collective-permute-start.8 = (f32[24,10,1,256]{3,0,2,1:T(8,128)}, f32[24,10,1,256]{3,0,2,1:T(8,128)}, u32[]{:S(2)}, u32[]{:S(2)}) collective-permute-start(f32[24,10,1,256]{3,0,2,1:T(8,128)} %get-tuple-element.313), channel_id=1, source_target_pairs={{0,1},{1,2},{2,3},{4,5},{5,6},{6,7},{8,9},{9,10},{10,11},{12,13},{... | collective-permute-start | bytes 737288 | tf_op jit(solution)/shard_map/ppermute | solution.py:19
  788.7 10.5 collective-permute-start.9
  1109.1 1.2 copy-start.8
  1111.9 2.7 copy-start.5
  1114.6 4.9 copy-start.14
  1114.6 48.9 %copy-start.15 = (f32[1,8,8]{1,2,0:T(8,128)S(1)}, f32[1,8,8]{1,2,0:T(8,128)}, u32[]{:S(2)}) copy-start(f32[1,8,8]{1,2,0:T(8,128)} %custom-call.15) | copy-start | bytes 772
  1169.6 1.4 copy-start.9
  1177.6 1.4 copy-start.3
  1179.9 1.6 copy-start.10
  1179.9 2.4 copy-start.11
  1182.4 3.0 copy-start.1
where the time goes:
time: 1200 us; the launch traced here: 1190 us
  local copies, waits for them, and re-layouts  611 us (51%)
  other arithmetic  297 us (25%)
  blocking collectives  83 us (7%)
  waiting for transfers between devices  78.4 us (7%)
  matrix products  70.8 us (6%)
  starting transfers between devices  42 us (4%)
    scatter-add x1, other arithmetic, body(): jnp.zeros((channels, volume), jnp.float32).at[:, flat_ids].add(contrib)  209 us
    while x162, local copies, waits for them, and re-layouts  141 us
    psum x2, blocking collectives, pair_sums(): lax.psum((gram_local(residual, residual), gram_local(residual, applied)),...  83 us
    all_to_all x1, waiting for transfers between devices, body(): lax.all_to_all(send_force, ('gz', 'gy'), split_axis=0, concat_axis=0, til...  71.3 us
    squeeze x36, local copies, waits for them, and re-layouts, plane_terms(): forces[corner_y * 2 + 1][:, start_y:start_y + width_rows, :]  62.3 us
    slice x72, local copies, waits for them, and re-layouts, shift_right(): return jnp.concatenate([filler, values[..., :-1]], axis=-1)  60.3 us
    reshape x18, local copies, waits for them, and re-layouts, plane_terms(): stacked = jnp.stack(corners, 0).reshape(24, load_count, -1)  46.7 us
    squeeze x36, local copies, waits for them, and re-layouts, plane_terms(): forces[corner_y * 2][:, start_y:start_y + width_rows, :]  45.4 us
  transfers between devices with their start and end apart: 12, of which 4 were waited for; matrix products, arithmetic and copies ran while one was open for 4% of the time, Pallas kernels for 0%

commit v1 on v0

v1 whole, which is shorter than its diff:
```python
import functools

import jax
import jax.numpy as jnp
import numpy as np
from jax import lax
from jax.experimental import pallas as pl
from jax.experimental.pallas import tpu as pltpu
from jax.sharding import PartitionSpec as P

LOADS = 8
ROWS = 24
SPRING = 0.5
SPLIT = 16
GROUP = 8
VMEM_LIMIT = 48 * 1024 * 1024

VMEM = pl.BlockSpec(memory_space=pltpu.VMEM)
SMEM = pl.BlockSpec(memory_space=pltpu.SMEM)
PARAMS = pltpu.CompilerParams(vmem_limit_bytes=VMEM_LIMIT)

_d, _l, _m = np.meshgrid(np.arange(8), np.arange(8), np.arange(8), indexing="ij")
DIAGONALS = ((_m - _l) % 8 == _d).astype(np.float32)


def to_diagonals(matrix):
    return jnp.sum(DIAGONALS * matrix[None], axis=1)


def from_diagonals(diagonals):
    return jnp.sum(DIAGONALS * diagonals[:, None, :], axis=0)


def spread(matrices, width):
    stacked = jnp.stack([to_diagonals(m) for m in matrices])
    return jnp.broadcast_to(stacked[..., None], stacked.shape + (width,))


def pack_kernel(capacity, owner_ref, live_ref, force_ref, voxel_ref, out_ref, count_ref):
    devices, rows, _, width = out_ref.shape
    blocks = owner_ref.shape[0]
    empty = jnp.full((8, width), -1.0, jnp.float32)
    zero = jnp.zeros((8, width), jnp.float32)

    def clear(dev, carry):
        count_ref[dev] = 0
        for row in range(rows):
            out_ref[dev, row] = zero if row < 3 * capacity else empty
        return carry

    lax.fori_loop(0, devices, clear, 0)
    lane = lax.broadcasted_iota(jnp.int32, (8, width), 1)
    sub = lax.broadcasted_iota(jnp.int32, (8, width), 0)

    def place(block, carry):
        owner = owner_ref[block]
        rank = count_ref[owner]
        count_ref[owner] = rank + 1
        limit = jnp.full((8, width), live_ref[block, 0], jnp.int32)
        for load in range(1, LOADS):
            limit = jnp.where(sub == load, live_ref[block, load], limit)
        keep = lane < limit
        for k in range(3):
            value = force_ref[block, k * 8 : k * 8 + 8, :]
            out_ref[owner, rank * 3 + k] = jnp.where(keep, value, 0.0)
        ids = voxel_ref[pl.ds(block, 1), :].astype(jnp.float32)
        out_ref[owner, 3 * capacity + rank // 8, pl.ds(rank % 8, 1), :] = ids
        return carry

    lax.fori_loop(0, blocks, place, 0)


def pack(owner, live, force, voxel, devices, capacity):
    rows = 3 * capacity + -(-capacity // 8)
    return pl.pallas_call(
        functools.partial(pack_kernel, capacity),
        out_shape=jax.ShapeDtypeStruct((devices, rows, 8, force.shape[2]), jnp.float32),
        in_specs=[SMEM, SMEM, VMEM, VMEM],
        out_specs=VMEM,
        scratch_shapes=[pltpu.SMEM((devices,), jnp.int32)],
        compiler_params=PARAMS,
    )(owner, live, force, voxel)


def scatter_kernel(capacity, width_x, valid_ref, got_ref, out_ref, left_ref, acc_ref, list_ref):
    devices, rows, _, width = got_ref.shape
    total = devices * capacity
    slots = GROUP * width
    cols = acc_ref.shape[2]
    tiles = acc_ref.shape[0]

    def gather(block, count):
        list_ref[count] = block
        return count + (valid_ref[block] > 0).astype(jnp.int32)

    count = lax.fori_loop(0, total, gather, jnp.int32(0))

    def clear(tile, carry):
        acc_ref[tile] = jnp.zeros(acc_ref.shape[1:], jnp.float32)
        return carry

    lax.fori_loop(0, tiles, clear, 0)
    column = lax.broadcasted_iota(jnp.int32, (cols, slots), 0)

    def step(index, carry):
        parts = []
        ids = []
        for j in range(GROUP):
            place = index * GROUP + j
            block = list_ref[jnp.where(place < count, place, 0)]
            dev = block // capacity
            slot = block % capacity
            parts.append(
                jnp.concatenate([got_ref[dev, slot * 3 + k] for k in range(3)], axis=0)
            )
            row = got_ref[dev, 3 * capacity + slot // 8, pl.ds(slot % 8, 1), :]
            ids.append(jnp.where(place < count, row, -1.0))
        values = jnp.concatenate(parts, axis=1)
        voxel = jnp.concatenate(ids, axis=1).astype(jnp.int32)
        high = values.astype(jnp.bfloat16).astype(jnp.float32)
        low = values - high
        both = jnp.concatenate([high, low], axis=0)
        line = lax.shift_right_arithmetic(voxel, 10)
        along = jnp.bitwise_and(voxel, tiles * cols - 1)
        for r in range(SPLIT):
            left_ref[r * 48 : r * 48 + 48, :] = jnp.where(line == r, both, 0.0).astype(
                jnp.bfloat16
            )

        def tile(t, inner):
            right = jnp.where(column == along - t * cols, 1.0, 0.0).astype(jnp.bfloat16)
            acc_ref[t] += lax.dot_general(
                left_ref[...],
                right,
                (((1,), (1,)), ((), ())),
                preferred_element_type=jnp.float32,
            )
            return inner

        lax.fori_loop(0, tiles, tile, 0)
        return carry

    lax.fori_loop(0, (count + GROUP - 1) // GROUP, step, 0)
    for r in range(SPLIT):
        for t in range(tiles):
            out_ref[r * tiles + t] = (
                acc_ref[t, r * 48 : r * 48 + 24, :] + acc_ref[t, r * 48 + 24 : r * 48 + 48, :]
            )


def scatter(got, capacity, depth, height, width_x):
    volume = depth * height * width_x
    tiles = volume // SPLIT // width_x
    assert volume // SPLIT == 1024
    first = got[:, 3 * capacity :, :, 0].reshape(got.shape[0], -1)[:, :capacity]
    valid = (first >= 0.0).astype(jnp.int32).reshape(-1)
    return pl.pallas_call(
        functools.partial(scatter_kernel, capacity, width_x),
        out_shape=jax.ShapeDtypeStruct((depth * height, ROWS, width_x), jnp.float32),
        in_specs=[SMEM, VMEM],
        out_specs=VMEM,
        scratch_shapes=[
            pltpu.VMEM((SPLIT * 48, GROUP * got.shape[3]), jnp.bfloat16),
            pltpu.VMEM((tiles, SPLIT * 48, width_x), jnp.float32),
            pltpu.SMEM((valid.shape[0] + 1,), jnp.int32),
        ],
        compiler_params=PARAMS,
    )(valid, got)


def shift_left(value):
    width = value.shape[-1]
    lane = lax.broadcasted_iota(jnp.int32, value.shape, 1)
    return jnp.where(lane == width - 1, 0.0, pltpu.roll(value, width - 1, 1))


def shift_right(value):
    lane = lax.broadcasted_iota(jnp.int32, value.shape, 1)
    return jnp.where(lane == 0, 0.0, pltpu.roll(value, 1, 1))


def mixed(value, coefficients):
    parts = []
    for k in range(3):
        piece = value[k * 8 : k * 8 + 8]
        total = piece * coefficients[0]
        for s in range(1, 8):
            total = total + pltpu.roll(piece, s, 0) * coefficients[s]
        parts.append(total)
    return jnp.concatenate(parts, axis=0)


def store_split(split_ref, z, y, value):
    both = jnp.concatenate([value, shift_left(value)], axis=0)
    high = both.astype(jnp.bfloat16)
    low = (both - high.astype(jnp.float32)).astype(jnp.bfloat16)
    split_ref[z, y, 0:48, :] = high
    split_ref[z, y, 48:96, :] = low


def run_operator(split_ref, field, weight_ref, weight_at, matrix_ref, out_ref, carry_ref):
    planes, lines = split_ref.shape[0] - 1, split_ref.shape[1] - 1
    matrix = matrix_ref[...]

    def plane(ze, carry):
        weights = weight_ref[ze + weight_at]
        before = None
        for ye in range(lines):
            corners = [split_ref.at[ze + a, ye + b] for a in (0, 1) for b in (0, 1)]
            high = jnp.concatenate([c[0:48, :] for c in corners], axis=0)
            low = jnp.concatenate([c[48:96, :] for c in corners], axis=0)
            forces = jnp.dot(
                matrix,
                jnp.concatenate([high, high, low], axis=0),
                preferred_element_type=jnp.float32,
            )
            forces = forces * weights[ye + weight_at : ye + weight_at + 1, :]
            if ye > 0:
                n = ye - 1
                lower = forces[0:48] + before[48:96] + carry_ref[n]
                carry_ref[n] = forces[96:144] + before[144:192]
                result = lower[0:24] + shift_right(lower[24:48])
                out_ref[ze, n] = result + SPRING * field(ze, ye)
            before = forces
        return carry

    carry_ref[...] = jnp.zeros(carry_ref.shape, jnp.float32)
    lax.fori_loop(0, planes, plane, 0)


def run_grams(first, second, depth, height, gram_ref):
    width = gram_ref.shape[-1]

    def plane(z, carry):
        sums = list(carry)
        for y in range(height):
            a = first(z, y)
            b = second(z, y)
            for k in range(3):
                a8 = a[k * 8 : k * 8 + 8]
                b8 = b[k * 8 : k * 8 + 8]
                for s in range(8):
                    rolled = a8 if s == 0 else pltpu.roll(a8, s, 0)
                    for h in range(0, a8.shape[1], width):
                        sums[s] = sums[s] + rolled[:, h : h + width] * a8[:, h : h + width]
                        sums[8 + s] = sums[8 + s] + rolled[:, h : h + width] * b8[:, h : h + width]
        return tuple(sums)

    sums = lax.fori_loop(0, depth, plane, tuple(jnp.zeros((8, width), jnp.float32) for _ in range(16)))
    for s in range(16):
        gram_ref[s // 8, s % 8] = sums[s]


def first_kernel(field_ref, weight_ref, matrix_ref, out_ref, gram_ref, split_ref, carry_ref):
    depth, lines = field_ref.shape[0], field_ref.shape[1]

    def split(z, carry):
        for y in range(lines):
            store_split(split_ref, z, y, field_ref[z, y])
        return carry

    lax.fori_loop(0, depth, split, 0)
    run_operator(
        split_ref, lambda z, y: field_ref[z, y], weight_ref, 0, matrix_ref, out_ref, carry_ref
    )
    run_grams(
        lambda z, y: field_ref[z + 2, y + 2],
        lambda z, y: out_ref[z + 2, y + 1],
        depth - 4,
        lines - 4,
        gram_ref,
    )


def second_kernel(
    inside_ref, coef_ref, field_ref, applied_ref, weight_ref, matrix_ref,
    res_ref, out_ref, gram_ref, split_ref, carry_ref, full_ref,
):
    depth, lines = full_ref.shape[0], full_ref.shape[1]

    def split(z, carry):
        coef = [coef_ref[0, s] for s in range(8)]
        for y in range(lines):
            value = field_ref[z + 1, y + 1] - mixed(applied_ref[z + 1, y], coef)
            value = value * inside_ref[z, y]
            full_ref[z, y] = value
            store_split(split_ref, z, y, value)
        return carry

    lax.fori_loop(0, depth, split, 0)
    run_operator(
        split_ref, lambda z, y: full_ref[z, y], weight_ref, 1, matrix_ref, out_ref, carry_ref
    )
    run_grams(
        lambda z, y: full_ref[z + 1, y + 1],
        lambda z, y: out_ref[z + 1, y],
        depth - 2,
        lines - 2,
        gram_ref,
    )

    def keep(z, carry):
        for y in range(lines - 2):
            res_ref[z, y] = full_ref[z + 1, y + 1]
        return carry

    lax.fori_loop(0, depth - 2, keep, 0)


def last_kernel(coef_ref, field_ref, res_ref, first_ref, second_ref, disp_ref, out_ref):
    depth, lines = res_ref.shape[0], res_ref.shape[1]

    def plane(z, carry):
        coefs = [[coef_ref[i, s] for s in range(8)] for i in range(3)]
        for y in range(lines):
            residual = res_ref[z, y]
            disp = mixed(field_ref[z + 2, y + 2], coefs[0]) + mixed(residual, coefs[1])
            left = residual - mixed(second_ref[z + 1, y], coefs[1])
            left = left - mixed(first_ref[z + 2, y + 1], coefs[2])
            disp_ref[:, z, y, :] = disp
            out_ref[:, z, y, :] = left
        return carry

    lax.fori_loop(0, depth, plane, 0)


def first_operator(field, weights, matrix):
    depth, lines, _, width = field.shape
    return pl.pallas_call(
        first_kernel,
        out_shape=(
            jax.ShapeDtypeStruct((depth - 1, lines - 2, ROWS, width), jnp.float32),
            jax.ShapeDtypeStruct((2, 8, 8, 128), jnp.float32),
        ),
        in_specs=[VMEM] * 3,
        out_specs=(VMEM, VMEM),
        scratch_shapes=[
            pltpu.VMEM((depth, lines, 96, width), jnp.bfloat16),
            pltpu.VMEM((lines - 2, 48, width), jnp.float32),
        ],
        compiler_params=PARAMS,
    )(field, weights, matrix)


def second_operator(inside, coef, field, applied, weights, matrix):
    depth, lines, _, width = field.shape
    depth, lines = depth - 2, lines - 2
    return pl.pallas_call(
        second_kernel,
        out_shape=(
            jax.ShapeDtypeStruct((depth - 2, lines - 2, ROWS, width), jnp.float32),
            jax.ShapeDtypeStruct((depth - 1, lines - 2, ROWS, width), jnp.float32),
            jax.ShapeDtypeStruct((2, 8, 8, 128), jnp.float32),
        ),
        in_specs=[SMEM] + [VMEM] * 5,
        out_specs=(VMEM, VMEM, VMEM),
        scratch_shapes=[
            pltpu.VMEM((depth, lines, 96, width), jnp.bfloat16),
            pltpu.VMEM((lines - 2, 48, width), jnp.float32),
            pltpu.VMEM((depth, lines, ROWS, width), jnp.float32),
        ],
        compiler_params=PARAMS,
    )(inside, coef, field, applied, weights, matrix)


def last_update(coef, field, residual, first, second):
    depth, lines, _, width = residual.shape
    shape = jax.ShapeDtypeStruct((ROWS, depth, lines, width), jnp.float32)
    return pl.pallas_call(
        last_kernel,
        out_shape=(shape, shape),
        in_specs=[VMEM] * 5,
        out_specs=(VMEM, VMEM),
        compiler_params=PARAMS,
    )(coef, field, residual, first, second)


def with_halo(block, axis, dim, below, above):
    count = lax.axis_size(axis)
    forward = [(i, i + 1) for i in range(count - 1)]
    backward = [(target, source) for source, target in forward]
    size = block.shape[dim]
    low = lax.ppermute(lax.slice_in_dim(block, size - below, None, axis=dim), axis, forward)
    high = lax.ppermute(lax.slice_in_dim(block, 0, above, axis=dim), axis, backward)
    return jnp.concatenate([low, block, high], axis=dim)


def solve_small(matrix, target):
    factor = jnp.linalg.cholesky(matrix)
    halfway = lax.linalg.triangular_solve(factor, target, left_side=True, lower=True)
    return lax.linalg.triangular_solve(
        factor, halfway, left_side=True, lower=True, transpose_a=True
    )


def total_grams(gram):
    sums = lax.psum(jnp.sum(gram, axis=-1), ("gz", "gy"))
    return from_diagonals(sums[0]), from_diagonals(sums[1])


def small_dot(a, b):
    return jnp.sum(a[:, :, None] * b[None, :, :], axis=1)


def body(patch_force, patch_owner, patch_voxel, patch_live, voxel_mask, element_matrix):
    depth, height, width = voxel_mask.shape
    groups_z = lax.axis_size("gz")
    groups_y = lax.axis_size("gy")
    devices = groups_z * groups_y
    blocks = patch_force.shape[0]
    capacity = max(2, (2 * blocks + devices - 1) // devices)

    packed = pack(patch_owner, patch_live, patch_force, patch_voxel, devices, capacity)
    got = lax.all_to_all(
        packed.reshape(devices, -1, packed.shape[3]), ("gz", "gy"), split_axis=0, concat_axis=0, tiled=True
    ).reshape(packed.shape)

    weights = with_halo(voxel_mask, "gz", 0, 2, 1)
    weights = with_halo(weights, "gy", 1, 2, 1).astype(jnp.float32)
    wide = jnp.kron(element_matrix, jnp.eye(LOADS, dtype=jnp.float32))
    high = wide.astype(jnp.bfloat16)
    low = (wide - lax.reduce_precision(wide, 8, 7)).astype(jnp.bfloat16)
    matrix = jnp.concatenate([high, low, high], axis=1)
    node_z = jnp.arange(depth + 2) - 1 + lax.axis_index("gz") * depth
    node_y = jnp.arange(height + 2) - 1 + lax.axis_index("gy") * height
    inside_z = (node_z >= 0) & (node_z < groups_z * depth)
    inside_y = (node_y >= 0) & (node_y < groups_y * height)
    inside = (inside_z[:, None] & inside_y[None, :]).astype(jnp.float32)

    force = scatter(got, capacity, depth, height, width).reshape(depth, height, ROWS, width)
    field = with_halo(force, "gz", 0, 2, 2)
    field = with_halo(field, "gy", 1, 2, 2)

    applied, gram = first_operator(field, weights, matrix)
    norm_gram, curvature = total_grams(gram)
    curvature = 0.5 * (curvature + curvature.T)
    alpha = solve_small(curvature, norm_gram)

    residual, again, gram = second_operator(
        inside, spread([alpha], width), field, applied, weights, matrix
    )
    norm_next, cross = total_grams(gram)
    beta = solve_small(norm_gram, norm_next)
    curvature = cross - small_dot(small_dot(beta.T, curvature), beta)
    curvature = 0.5 * (curvature + curvature.T)
    alpha_next = solve_small(curvature, norm_next)
    joint = small_dot(beta, alpha_next)

    coef = spread([alpha + joint, alpha_next, joint], width)
    return last_update(coef, field, residual, applied, again)


def solution(mesh):
    placed = (
        P(("gz", "gy"), None, None),
        P(("gz", "gy")),
        P(("gz", "gy"), None),
        P(("gz", "gy"), None),
        P("gz", "gy", None),
        P(),
    )
    return jax.shard_map(
        body,
        mesh=mesh,
        in_specs=placed,
        out_specs=(P(None, "gz", "gy", None), P(None, "gz", "gy", None)),
        check_vma=False,
    )
```

time: 1200 us -> 329 us (0.27); the launches traced: 1190 us -> 328 us
  local copies, waits for them, and re-layouts: 611 us -> 17 us
  other arithmetic: 297 us -> 13.3 us
  Pallas kernels: 0 us -> 78.2 us
  matrix products: 70.8 us -> 0.98 us
  blocking collectives: 83 us -> 99.2 us
    scatter-add x1 -> x0, other arithmetic: 209 us -> none  [body(): jnp.zeros((channels, volume), jnp.float32).at[:, flat_ids].add(contrib)]
    slice x317 -> x5, local copies, waits for them, and re-layouts: 164 us -> 0.84 us  [the longest x3 0.83 us: with_halo(): lax.slice_in_dim(block, size - below, None, axis=dim)]
    while x162 -> x0, local copies, waits for them, and re-layouts: 141 us -> none
    squeeze x154 -> x0, local copies, waits for them, and re-layouts: 125 us -> none  [the longest x36 62.3 us: plane_terms(): forces[corner_y * 2 + 1][:, start_y:start_y + width_rows, :]]
    pallas_call x0 -> x5, Pallas kernels: none -> 78.2 us  [the longest x1 30.2 us: scatter(): pl.pallas_call(functools.partial(scatter_kernel, capacity, width_x), out_...]
    reshape x24 -> x0, local copies, waits for them, and re-layouts: 72.7 us -> none  [the longest x18 46.7 us: plane_terms(): stacked = jnp.stack(corners, 0).reshape(24, load_count, -1)]
    dot_general x30 -> x0, matrix products: 69.7 us -> none  [the longest x18 37.5 us: plane_terms(): jnp.einsum('ij,jlq->ilq', element_matrix, stacked, precision=highest)]
    broadcast_in_dim x36 -> x0, other arithmetic: 55.9 us -> none  [the longest x18 36.1 us: one_plane(): lower_part[:, None]]
  transfers between devices with their start and end apart: 12 -> 9, of which waited for: 4 -> 4; matrix products, arithmetic and copies ran while one was open for 4% -> 2% of each run, Pallas kernels for 0% -> 9%
where the time goes in v1:
time: 329 us; the launch traced here: 328 us
  blocking collectives  99.2 us (30%)
  waiting for transfers between devices  81 us (25%)
  Pallas kernels  78.2 us (24%)
  starting transfers between devices  37.3 us (11%)
  local copies, waits for them, and re-layouts  17 us (5%)
  other arithmetic  13.3 us (4%)
    psum x2, blocking collectives, total_grams(): sums = lax.psum(jnp.sum(gram, axis=-1), ('gz', 'gy'))  99.2 us
    all_to_all x1, waiting for transfers between devices, body(): lax.all_to_all(packed.reshape(devices, -1, packed.shape[3]), ('gz', 'gy')...  68.4 us
    pallas_call x1, Pallas kernels, scatter(): pl.pallas_call(functools.partial(scatter_kernel, capacity, width_x), out_...  30.2 us
    ppermute x4, starting transfers between devices, with_halo(): lax.ppermute(lax.slice_in_dim(block, size - below, None, axis=dim), axis,...  24.9 us
    pallas_call x1, Pallas kernels, first_operator(): pl.pallas_call(first_kernel, out_shape=(jax.ShapeDtypeStruct((depth - 1,...  17.5 us
    pallas_call x1, Pallas kernels, second_operator(): pl.pallas_call(second_kernel, out_shape=(jax.ShapeDtypeStruct((depth - 2,...  16.1 us
    unnamed x27, local copies, waits for them, and re-layouts  13.2 us
    pallas_call x1, Pallas kernels, last_update(): pl.pallas_call(last_kernel, out_shape=(shape, shape), in_specs=[VMEM] * 5...  10.1 us
  transfers between devices with their start and end apart: 9, of which 4 were waited for; matrix products, arithmetic and copies ran while one was open for 2% of the time, Pallas kernels for 9%

profile of v1, /device:TPU:0, one launch (start us, length us, event | category | flops | bytes accessed | tf_op | source)
XLA Modules:
  0.0 328.1 jit_solution(10118047260223086210)
XLA Ops:
  0.6 0.8 copy.37.live_ref
  1.4 1.4 copy-done.6
  2.8 0.8 copy-done.7
  3.7 0.7 copy-done.8
  4.3 4.2 %shard_map.86 = f32[32,25,8,128]{3,2,1,0:T(8,128)S(1)} custom-call(s32[128]{0:T(128)S(1)} %copy-done.8, s32[128,8]{1,0:T(8,128)S(1)} %copy.37.live_ref, f32[128,24,128]{2,1,0:T(8,128)S(1)} %copy-done.6, s32[128,128]{1,0:T(8,128)S(1)} %copy-done.7), custom_call_target="tpu_custom_call" | custom-call | tf_op jit(solution)/shard_map/pallas_call | solution.py:75
  8.5 1.7 copy-done.2
  10.2 7.3 %all-to-all-start = ((f32[32,200,128]{2,1,0:T(8,128)}), f32[32,200,128]{2,1,0:T(8,128)S(1)}, u32[]{:S(2)}, u32[]{:S(2)}) async-start(f32[32,200,128]{2,1,0:T(8,128)} %bitcast.82), calls=%async_computation | async-start | bytes 6553600 | tf_op jit(solution)/shard_map/all_to_all | solution.py:414
  17.5 1.3 collective-permute-start.5
  18.8 4.5 %collective-permute-start.4 = (s32[2,8,256]{2,1,0:T(8,128)S(1)}, s32[2,8,256]{2,1,0:T(8,128)S(1)}, u32[]{:S(2)}, u32[]{:S(2)}) collective-permute-start(s32[2,8,256]{2,1,0:T(8,128)S(1)} %slice.60), channel_id=1, source_target_pairs={{0,4},{4,8},{8,12},{12,16},{16,20},{20,24},{24,28},{1,5},{5,9},{9,... | collective-permute-start | bytes 49160 | tf_op jit(solution)/shard_map/ppermute | solution.py:383
  23.4 68.4 %all-to-all-done = f32[32,200,128]{2,1,0:T(8,128)S(1)} async-done(((f32[32,200,128]{2,1,0:T(8,128)}), f32[32,200,128]{2,1,0:T(8,128)S(1)}, u32[]{:S(2)}, u32[]{:S(2)}) %all-to-all-start) | async-done | bytes 3276832 | tf_op jit(solution)/shard_map/all_to_all | solution.py:414
  91.9 0.6 convert_reduce_fusion
  92.5 1.7 copy-done
  94.3 1.9 copy-done.1
  96.2 30.2 %shard_map.87 = f32[64,24,256]{2,1,0:T(8,128)S(1)} custom-call(s32[256]{0:T(256)S(1)} %reshape.96.valid_ref, f32[32,25,8,128]{3,2,1,0:T(8,128)S(1)} %bitcast.81), custom_call_target="tpu_custom_call" | custom-call | tf_op jit(solution)/shard_map/pallas_call | solution.py:157
  126.4 0.8 fusion.22
  127.2 1.3 collective-permute-start.1
  128.5 14.7 %collective-permute-start = (f32[2,8,24,256]{3,2,1,0:T(8,128)S(1)}, f32[2,8,24,256]{3,2,1,0:T(8,128)S(1)}, u32[]{:S(2)}, u32[]{:S(2)}) collective-permute-start(f32[2,8,24,256]{3,2,1,0:T(8,128)S(1)} %bitcast.83), channel_id=1, source_target_pairs={{0,4},{4,8},{8,12},{12,16},{16,20},{20,24},{24,28},{1,5},{5,9},{9,... | collective-permute-start | bytes 1179656 | tf_op jit(solution)/shard_map/ppermute | solution.py:383
  143.2 1.6 broadcast_multiply_fusion
  144.8 2.3 mul.148
  147.2 3.1 collective-permute-done.1
  150.4 8.7 %collective-permute-done = f32[2,8,24,256]{3,2,1,0:T(8,128)S(1)} collective-permute-done((f32[2,8,24,256]{3,2,1,0:T(8,128)S(1)}, f32[2,8,24,256]{3,2,1,0:T(8,128)S(1)}, u32[]{:S(2)}, u32[]{:S(2)}) %collective-permute-start) | collective-permute-done | bytes 393248 | tf_op jit(solution)/shard_map/ppermute | solution.py:383
  159.1 2.0 collective-permute-start.2
  161.1 1.3 collective-permute-start.3
  162.5 1.3 collective-permute-start.7
  163.8 3.7 %collective-permute-start.6 = (s32[11,2,256]{2,1,0:T(2,128)S(1)}, s32[11,2,256]{2,1,0:T(2,128)S(1)}, u32[]{:S(2)}, u32[]{:S(2)}) collective-permute-start(s32[11,2,256]{2,1,0:T(2,128)S(1)} %slice.71), channel_id=1, source_target_pairs={{0,1},{1,2},{2,3},{4,5},{5,6},{6,7},{8,9},{9,10},{10,11},{12,13},{... | collective-permute-start | bytes 67592 | tf_op jit(solution)/shard_map/ppermute | solution.py:383
  167.6 0.7 collective-permute-done.6
  168.4 2.1 pad_maximum_fusion.field_ref
  170.5 17.5 %shard_map.88 = (f32[11,10,24,256]{3,2,1,0:T(8,128)S(1)}, f32[2,8,8,128]{3,2,1,0:T(8,128)S(1)}) custom-call(f32[12,12,24,256]{3,2,1,0:T(8,128)} %pad_maximum_fusion.field_ref, f32[11,11,256]{2,1,0:T(8,128)S(1)} %add_convert_fusion.weight_ref, bf16[192,576]{1,0:T(8,128)(2,1)S(1)} %pad_maximum_fusion.4.matrix_ref), custom_call_target="tpu_custom_call" | custom-call | tf_op jit(solution)/shard_map/pallas_call | solution.py:329
  188.1 1.5 copy-done.3
  189.7 57.0 %psum.14 = f32[2,8,8]{2,1,0:T(8,128)S(1)} all-reduce(f32[2,8,8]{2,1,0:T(8,128)S(1)} %reduce_sum.117), channel_id=1, replica_groups=mesh['gz'=8,'gy'=4] {'gz','gy'}, use_global_device_ids=true, to_apply=%region_1.2 | all-reduce | flops 128 | bytes 1024 | tf_op jit(solution)/shard_map/psum | solution.py:397
  246.9 0.7 cholesky.59
  247.6 0.6 compare_reduce_fusion.2
  248.3 0.6 fusion.1
  248.9 0.6 custom-call.13
  250.0 0.7 cholesky.70
  250.8 0.6 compare_reduce_fusion.1
  251.4 0.6 fusion.2
  252.1 0.6 custom-call.15
  252.8 16.1 %shard_map.89 = (f32[8,8,24,256]{3,2,1,0:T(8,128)S(1)}, f32[9,8,24,256]{3,2,1,0:T(8,128)S(1)}, f32[2,8,8,128]{3,2,1,0:T(8,128)S(1)}) custom-call(f32[10,10]{1,0:T(8,128)S(1)} %and_convert_fusion.inside_ref, f32[1,8,8,256]{3,2,1,0:T(8,128)S(1)} %broadcast_in_dim.9.coef_ref, f32[12,12,24,256]{3,2,1,0:T(8,128)} %pad_maximum_fusion.field_ref, ...), custom_call_target="tpu_custom_call" | custom-call | tf_op jit(solution)/shard_map/pallas_call | solution.py:348
  268.9 1.2 copy-done.4
  270.2 42.2 %psum.15 = f32[2,8,8]{2,1,0:T(8,128)S(1)} all-reduce(f32[2,8,8]{2,1,0:T(8,128)S(1)} %reduce_sum.121), channel_id=1, replica_groups=mesh['gz'=8,'gy'=4] {'gz','gy'}, use_global_device_ids=true, to_apply=%region_8.12 | all-reduce | flops 128 | bytes 1024 | tf_op jit(solution)/shard_map/psum | solution.py:397
  313.2 0.7 cholesky.81
  313.9 0.6 compare_reduce_fusion
  314.6 0.6 fusion.3
  315.2 0.6 custom-call.17
  315.8 0.2 fusion.4
  316.4 1.5 copy-done.5
  317.9 10.1 %shard_map.90 = (f32[24,8,8,256]{3,2,1,0:T(8,128)}, f32[24,8,8,256]{3,2,1,0:T(8,128)}) custom-call(f32[3,8,8,256]{3,2,1,0:T(8,128)S(1)} %broadcast_in_dim.10.coef_ref, f32[12,12,24,256]{3,2,1,0:T(8,128)} %pad_maximum_fusion.field_ref, f32[8,8,24,256]{3,2,1,0:T(8,128)S(1)} %get-tuple-element.13.res_ref, f32[11,10,24,256]{3,2,1,0:T(8,128)} %copy-done.3, ...), custom_call_target="tpu_custom_call" | custom-call | tf_op jit(solution)/shard_map/pallas_call | solution.py:369
  (70 shorter events, 2.6 us)
Async XLA Ops:
  1.4 1.4 copy-start.6
  2.8 0.8 copy-start.7
  3.7 0.7 copy-start.8
  8.5 1.7 copy-start.2
  10.2 7.3 %copy-start.10 = (s32[8,8,256]{2,1,0:T(8,128)S(1)}, s32[8,8,256]{2,1,0:T(8,128)}, u32[]{:S(2)}) copy-start(s32[8,8,256]{2,1,0:T(8,128)} %param.16) | copy-start | bytes 196612
  10.2 81.6 %all-to-all-start = ((f32[32,200,128]{2,1,0:T(8,128)}), f32[32,200,128]{2,1,0:T(8,128)S(1)}, u32[]{:S(2)}, u32[]{:S(2)}) async-start(f32[32,200,128]{2,1,0:T(8,128)} %bitcast.82), calls=%async_computation | async-start | bytes 6553600 | tf_op jit(solution)/shard_map/all_to_all | solution.py:414
  17.5 145.0 %collective-permute-start.5 = (s32[1,8,256]{2,1,0:T(8,128)S(1)}, s32[1,8,256]{2,1,0:T(8,128)S(1)}, u32[]{:S(2)}, u32[]{:S(2)}) collective-permute-start(s32[1,8,256]{2,1,0:T(8,128)S(1)} %slice.61), channel_id=1, source_target_pairs={{4,0},{8,4},{12,8},{16,12},{20,16},{24,20},{28,24},{5,1},{9,5},{13... | collective-permute-start | bytes 24584 | tf_op jit(solution)/shard_map/ppermute | solution.py:384
  18.8 143.6 %collective-permute-start.4 = (s32[2,8,256]{2,1,0:T(8,128)S(1)}, s32[2,8,256]{2,1,0:T(8,128)S(1)}, u32[]{:S(2)}, u32[]{:S(2)}) collective-permute-start(s32[2,8,256]{2,1,0:T(8,128)S(1)} %slice.60), channel_id=1, source_target_pairs={{0,4},{4,8},{8,12},{12,16},{16,20},{20,24},{24,28},{1,5},{5,9},{9,... | collective-permute-start | bytes 49160 | tf_op jit(solution)/shard_map/ppermute | solution.py:383
  92.5 1.7 copy-start
  94.2 1.9 copy-start.1
  96.2 47.0 %copy-start.11 = (f32[24,24]{1,0:T(8,128)S(1)}, f32[24,24]{1,0:T(8,128)}, u32[]{:S(2)}) copy-start(f32[24,24]{1,0:T(8,128)} %param.17) | copy-start | bytes 6916
  127.2 23.2 %collective-permute-start.1 = (f32[2,8,24,256]{3,2,1,0:T(8,128)}, f32[2,8,24,256]{3,2,1,0:T(8,128)S(1)}, u32[]{:S(2)}, u32[]{:S(2)}) collective-permute-start(f32[2,8,24,256]{3,2,1,0:T(8,128)} %bitcast.4), channel_id=1, source_target_pairs={{4,0},{8,4},{12,8},{16,12},{20,16},{24,20},{28,24},{5,1},{9,5},{13... | collective-permute-start | bytes 1179656 | tf_op jit(solution)/shard_map/ppermute | solution.py:384
  128.5 30.6 %collective-permute-start = (f32[2,8,24,256]{3,2,1,0:T(8,128)S(1)}, f32[2,8,24,256]{3,2,1,0:T(8,128)S(1)}, u32[]{:S(2)}, u32[]{:S(2)}) collective-permute-start(f32[2,8,24,256]{3,2,1,0:T(8,128)S(1)} %bitcast.83), channel_id=1, source_target_pairs={{0,4},{4,8},{8,12},{12,16},{16,20},{20,24},{24,28},{1,5},{5,9},{9,... | collective-permute-start | bytes 1179656 | tf_op jit(solution)/shard_map/ppermute | solution.py:383
  159.1 9.3 %collective-permute-start.2 = (f32[12,2,24,256]{3,2,1,0:T(8,128)S(1)}, f32[12,2,24,256]{3,2,1,0:T(8,128)S(1)}, u32[]{:S(2)}, u32[]{:S(2)}) collective-permute-start(f32[12,2,24,256]{3,2,1,0:T(8,128)S(1)} %get-tuple-element.22), channel_id=1, source_target_pairs={{0,1},{1,2},{2,3},{4,5},{5,6},{6,7},{8,9},{9,10},{10,11},{12,13},{... | collective-permute-start | bytes 1769480 | tf_op jit(solution)/shard_map/ppermute | solution.py:383
  161.1 7.3 %collective-permute-start.3 = (f32[12,2,24,256]{3,2,1,0:T(8,128)S(1)}, f32[12,2,24,256]{3,2,1,0:T(8,128)S(1)}, u32[]{:S(2)}, u32[]{:S(2)}) collective-permute-start(f32[12,2,24,256]{3,2,1,0:T(8,128)S(1)} %get-tuple-element.23), channel_id=1, source_target_pairs={{1,0},{2,1},{3,2},{5,4},{6,5},{7,6},{9,8},{10,9},{11,10},{13,12},{... | collective-permute-start | bytes 1769480 | tf_op jit(solution)/shard_map/ppermute | solution.py:384
  162.5 5.1 %collective-permute-start.7 = (s32[11,1,256]{2,1,0:T(1,128)S(1)}, s32[11,1,256]{2,1,0:T(1,128)S(1)}, u32[]{:S(2)}, u32[]{:S(2)}) collective-permute-start(s32[11,1,256]{2,1,0:T(1,128)S(1)} %slice.72), channel_id=1, source_target_pairs={{1,0},{2,1},{3,2},{5,4},{6,5},{7,6},{9,8},{10,9},{11,10},{13,12},{... | collective-permute-start | bytes 33800 | tf_op jit(solution)/shard_map/ppermute | solution.py:384
  163.8 4.5 %collective-permute-start.6 = (s32[11,2,256]{2,1,0:T(2,128)S(1)}, s32[11,2,256]{2,1,0:T(2,128)S(1)}, u32[]{:S(2)}, u32[]{:S(2)}) collective-permute-start(s32[11,2,256]{2,1,0:T(2,128)S(1)} %slice.71), channel_id=1, source_target_pairs={{0,1},{1,2},{2,3},{4,5},{5,6},{6,7},{8,9},{9,10},{10,11},{12,13},{... | collective-permute-start | bytes 67592 | tf_op jit(solution)/shard_map/ppermute | solution.py:383
  170.5 76.2 %copy-start.9 = (f32[8,8,8]{2,1,0:T(8,128)S(1)}, f32[8,8,8]{2,1,0:T(8,128)}, u32[]{:S(2)}) copy-start(f32[8,8,8]{2,1,0:T(8,128)} %constant.59.clone) | copy-start | bytes 6148
  188.1 1.5 copy-start.3
  268.9 1.2 copy-start.4
  316.4 1.5 copy-start.5

commit v2 on v1

--- a/solution.py
+++ b/solution.py
@@ -36,16 +36,17 @@
     return jnp.broadcast_to(stacked[..., None], stacked.shape + (width,))
 
 
-def pack_kernel(capacity, owner_ref, live_ref, force_ref, voxel_ref, out_ref, count_ref):
-    devices, rows, _, width = out_ref.shape
+def pack_kernel(shares, owner_ref, live_ref, force_ref, voxel_ref, near_ref, far_ref, count_ref):
     blocks = owner_ref.shape[0]
+    devices, _, _, width = near_ref.shape
     empty = jnp.full((8, width), -1.0, jnp.float32)
     zero = jnp.zeros((8, width), jnp.float32)
 
     def clear(dev, carry):
         count_ref[dev] = 0
-        for row in range(rows):
-            out_ref[dev, row] = zero if row < 3 * capacity else empty
+        for out_ref, share in zip((near_ref, far_ref), shares):
+            for row in range(out_ref.shape[1]):
+                out_ref[dev, row] = zero if row < 3 * share else empty
         return carry
 
     lax.fori_loop(0, devices, clear, 0)
@@ -60,29 +61,46 @@
         for load in range(1, LOADS):
             limit = jnp.where(sub == load, live_ref[block, load], limit)
         keep = lane < limit
-        for k in range(3):
-            value = force_ref[block, k * 8 : k * 8 + 8, :]
-            out_ref[owner, rank * 3 + k] = jnp.where(keep, value, 0.0)
+        values = [
+            jnp.where(keep, force_ref[block, k * 8 : k * 8 + 8, :], 0.0) for k in range(3)
+        ]
         ids = voxel_ref[pl.ds(block, 1), :].astype(jnp.float32)
-        out_ref[owner, 3 * capacity + rank // 8, pl.ds(rank % 8, 1), :] = ids
+
+        def store(out_ref, share, slot):
+            for k in range(3):
+                out_ref[owner, slot * 3 + k] = values[k]
+            out_ref[owner, 3 * share + slot // 8, pl.ds(slot % 8, 1), :] = ids
+
+        @pl.when(rank < shares[0])
+        def _():
+            store(near_ref, shares[0], rank)
+
+        @pl.when(rank >= shares[0])
+        def _():
+            store(far_ref, shares[1], rank - shares[0])
+
         return carry
 
     lax.fori_loop(0, blocks, place, 0)
 
 
-def pack(owner, live, force, voxel, devices, capacity):
-    rows = 3 * capacity + -(-capacity // 8)
+def pack(owner, live, force, voxel, devices, shares):
     return pl.pallas_call(
-        functools.partial(pack_kernel, capacity),
-        out_shape=jax.ShapeDtypeStruct((devices, rows, 8, force.shape[2]), jnp.float32),
+        functools.partial(pack_kernel, shares),
+        out_shape=tuple(
+            jax.ShapeDtypeStruct((devices, 3 * c + -(-c // 8), 8, force.shape[2]), jnp.float32)
+            for c in shares
+        ),
         in_specs=[SMEM, SMEM, VMEM, VMEM],
-        out_specs=VMEM,
+        out_specs=(VMEM, VMEM),
         scratch_shapes=[pltpu.SMEM((devices,), jnp.int32)],
         compiler_params=PARAMS,
     )(owner, live, force, voxel)
 
 
-def scatter_kernel(capacity, width_x, valid_ref, got_ref, out_ref, left_ref, acc_ref, list_ref):
+def scatter_kernel(capacity, valid_ref, got_ref, *refs):
+    before_ref = refs[0] if len(refs) == 5 else None
+    out_ref, left_ref, acc_ref, list_ref = refs[-4:]
     devices, rows, _, width = got_ref.shape
     total = devices * capacity
     slots = GROUP * width
@@ -143,29 +161,36 @@
     lax.fori_loop(0, (count + GROUP - 1) // GROUP, step, 0)
     for r in range(SPLIT):
         for t in range(tiles):
-            out_ref[r * tiles + t] = (
-                acc_ref[t, r * 48 : r * 48 + 24, :] + acc_ref[t, r * 48 + 24 : r * 48 + 48, :]
-            )
-
-
-def scatter(got, capacity, depth, height, width_x):
+            high = acc_ref[t, r * 48 : r * 48 + 24, :]
+            result = high + acc_ref[t, r * 48 + 24 : r * 48 + 48, :]
+            if before_ref is not None:
+                result = result + before_ref[r * tiles + t]
+            out_ref[r * tiles + t] = result
+
+
+def scatter(got, capacity, depth, height, width_x, before=None):
     volume = depth * height * width_x
     tiles = volume // SPLIT // width_x
     assert volume // SPLIT == 1024
     first = got[:, 3 * capacity :, :, 0].reshape(got.shape[0], -1)[:, :capacity]
     valid = (first >= 0.0).astype(jnp.int32).reshape(-1)
+    arrays = (valid, got) if before is None else (valid, got, before)
+    slots = got.shape[0] * capacity * got.shape[3]
     return pl.pallas_call(
-        functools.partial(scatter_kernel, capacity, width_x),
+        functools.partial(scatter_kernel, capacity),
         out_shape=jax.ShapeDtypeStruct((depth * height, ROWS, width_x), jnp.float32),
-        in_specs=[SMEM, VMEM],
+        in_specs=[SMEM] + [VMEM] * (len(arrays) - 1),
         out_specs=VMEM,
+        cost_estimate=pl.CostEstimate(
+            flops=4 * SPLIT * 48 * 1024 * slots, bytes_accessed=4 * got.size, transcendentals=0
+        ),
         scratch_shapes=[
             pltpu.VMEM((SPLIT * 48, GROUP * got.shape[3]), jnp.bfloat16),
             pltpu.VMEM((tiles, SPLIT * 48, width_x), jnp.float32),
             pltpu.SMEM((valid.shape[0] + 1,), jnp.int32),
         ],
         compiler_params=PARAMS,
-    )(valid, got)
+    )(*arrays)
 
 
 def shift_left(value):
@@ -229,7 +254,7 @@
 
 
 def run_grams(first, second, depth, height, gram_ref):
-    width = gram_ref.shape[-1]
+    width = gram_ref.shape[1]
 
     def plane(z, carry):
         sums = list(carry)
@@ -247,8 +272,11 @@
         return tuple(sums)
 
     sums = lax.fori_loop(0, depth, plane, tuple(jnp.zeros((8, width), jnp.float32) for _ in range(16)))
+    lane = lax.broadcasted_iota(jnp.int32, (8, width), 1)
+    tile = jnp.zeros((8, width), jnp.float32)
     for s in range(16):
-        gram_ref[s // 8, s % 8] = sums[s]
+        tile = jnp.where(lane == s, jnp.sum(sums[s], axis=1, keepdims=True), tile)
+    gram_ref[...] = tile
 
 
 def first_kernel(field_ref, weight_ref, matrix_ref, out_ref, gram_ref, split_ref, carry_ref):
@@ -330,7 +358,7 @@
         first_kernel,
         out_shape=(
             jax.ShapeDtypeStruct((depth - 1, lines - 2, ROWS, width), jnp.float32),
-            jax.ShapeDtypeStruct((2, 8, 8, 128), jnp.float32),
+            jax.ShapeDtypeStruct((8, 128), jnp.float32),
         ),
         in_specs=[VMEM] * 3,
         out_specs=(VMEM, VMEM),
@@ -350,7 +378,7 @@
         out_shape=(
             jax.ShapeDtypeStruct((depth - 2, lines - 2, ROWS, width), jnp.float32),
             jax.ShapeDtypeStruct((depth - 1, lines - 2, ROWS, width), jnp.float32),
-            jax.ShapeDtypeStruct((2, 8, 8, 128), jnp.float32),
+            jax.ShapeDtypeStruct((8, 128), jnp.float32),
         ),
         in_specs=[SMEM] + [VMEM] * 5,
         out_specs=(VMEM, VMEM, VMEM),
@@ -393,9 +421,158 @@
     )
 
 
-def total_grams(gram):
-    sums = lax.psum(jnp.sum(gram, axis=-1), ("gz", "gy"))
-    return from_diagonals(sums[0]), from_diagonals(sums[1])
+def reduce_kernel(counts, tile_ref, out_ref, line_ref, plane_ref, mid_ref, send_sems, recv_sems):
+    nz, ny = counts
+    gz, gy = lax.axis_index("gz"), lax.axis_index("gy")
+    beside = [(gz, lax.rem(gy + d, ny)) for d in range(1, ny)]
+    along = [(lax.rem(gz + d, nz), gy) for d in range(1, nz)]
+    barrier = pltpu.get_barrier_semaphore()
+    for peer in beside + along:
+        pl.semaphore_signal(barrier, inc=1, device_id=peer, device_id_type=pl.DeviceIdType.MESH)
+    pl.semaphore_wait(barrier, ny + nz - 2)
+
+    def exchange(source_ref, slots_ref, place, peers, first):
+        copies = [
+            pltpu.make_async_remote_copy(
+                src_ref=source_ref,
+                dst_ref=slots_ref.at[place],
+                send_sem=send_sems.at[first + i],
+                recv_sem=recv_sems.at[first + i],
+                device_id=peer,
+                device_id_type=pl.DeviceIdType.MESH,
+            )
+            for i, peer in enumerate(peers)
+        ]
+        for copy in copies:
+            copy.start()
+        slots_ref[place] = source_ref[...]
+        for copy in copies:
+            copy.wait()
+        total = slots_ref[0]
+        for i in range(1, slots_ref.shape[0]):
+            total = total + slots_ref[i]
+        return total
+
+    mid_ref[...] = exchange(tile_ref, line_ref, gy, beside, 0)
+    out_ref[...] = exchange(mid_ref, plane_ref, gz, along, ny - 1)
+
+
+def total_grams(tile):
+    nz, ny = lax.axis_size("gz"), lax.axis_size("gy")
+    sums = pl.pallas_call(
+        functools.partial(reduce_kernel, (nz, ny)),
+        out_shape=jax.ShapeDtypeStruct(tile.shape, jnp.float32),
+        in_specs=[VMEM],
+        out_specs=VMEM,
+        scratch_shapes=[
+            pltpu.VMEM((ny,) + tile.shape, jnp.float32),
+            pltpu.VMEM((nz,) + tile.shape, jnp.float32),
+            pltpu.VMEM(tile.shape, jnp.float32),
+            pltpu.SemaphoreType.DMA((ny + nz - 2,)),
+            pltpu.SemaphoreType.DMA((ny + nz - 2,)),
+        ],
+        compiler_params=pltpu.CompilerParams(collective_id=0, has_side_effects=True),
+    )(tile)
+    sums = sums[:, :16].T
+    return from_diagonals(sums[:8]), from_diagonals(sums[8:])
+
+
+def halo_kernel(counts, halo, field_ref, out_ref, send_sems, recv_sems):
+    nz, ny = counts
+    depth, lines = field_ref.shape[:2]
+    gz, gy = lax.axis_index("gz"), lax.axis_index("gy")
+    ways = [(dz, dy) for dz in (-1, 0, 1) for dy in (-1, 0, 1) if (dz, dy) != (0, 0)]
+
+    def exists(dz, dy):
+        z, y = gz + dz, gy + dy
+        return (z >= 0) & (z < nz) & (y >= 0) & (y < ny)
+
+    def source(step, size):
+        return {-1: pl.ds(0, halo), 0: pl.ds(0, size), 1: pl.ds(size - halo, halo)}[step]
+
+    def target(step, size):
+        return {-1: pl.ds(halo + size, halo), 0: pl.ds(halo, size), 1: pl.ds(0, halo)}[step]
+
+    def copy(i, sign):
+        dz, dy = ways[i]
+        return pltpu.make_async_remote_copy(
+            src_ref=field_ref.at[source(dz, depth), source(dy, lines)],
+            dst_ref=out_ref.at[target(dz, depth), target(dy, lines)],
+            send_sem=send_sems.at[i],
+            recv_sem=recv_sems.at[i],
+            device_id=(gz + sign * dz, gy + sign * dy),
+            device_id_type=pl.DeviceIdType.MESH,
+        )
+
+    barrier = pltpu.get_barrier_semaphore()
+    peers = jnp.int32(0)
+    for dz, dy in ways:
+        peers = peers + jnp.where(exists(dz, dy), 1, 0)
+
+        @pl.when(exists(dz, dy))
+        def _():
+            pl.semaphore_signal(
+                barrier, inc=1, device_id=(gz + dz, gy + dy), device_id_type=pl.DeviceIdType.MESH
+            )
+
+    pl.semaphore_wait(barrier, peers)
+    for i, (dz, dy) in enumerate(ways):
+
+        @pl.when(exists(dz, dy))
+        def _():
+            copy(i, 1).start()
+
+    def keep(z, carry):
+        for y in range(lines):
+            out_ref[z + halo, y + halo] = field_ref[z, y]
+        return carry
+
+    lax.fori_loop(0, depth, keep, 0)
+    for dz, dy in ways:
+
+        @pl.when(jnp.logical_not(exists(-dz, -dy)))
+        def _():
+            zs, ys = target(dz, depth), target(dy, lines)
+
+            def clear(z, carry):
+                for y in range(ys.size):
+                    out_ref[zs.start + z, ys.start + y] = jnp.zeros(out_ref.shape[2:], jnp.float32)
+                return carry
+
+            lax.fori_loop(0, zs.size, clear, 0)
+
+    for i, (dz, dy) in enumerate(ways):
+
+        @pl.when(exists(dz, dy))
+        def _():
+            copy(i, 1).wait_send()
+
+        @pl.when(exists(-dz, -dy))
+        def _():
+            copy(i, -1).wait_recv()
+
+
+def field_with_halo(field, halo):
+    depth, lines, rows, width = field.shape
+    counts = (lax.axis_size("gz"), lax.axis_size("gy"))
+    return pl.pallas_call(
+        functools.partial(halo_kernel, counts, halo),
+        out_shape=jax.ShapeDtypeStruct(
+            (depth + 2 * halo, lines + 2 * halo, rows, width), jnp.float32
+        ),
+        in_specs=[VMEM],
+        out_specs=VMEM,
+        scratch_shapes=[pltpu.SemaphoreType.DMA((8,)), pltpu.SemaphoreType.DMA((8,))],
+        compiler_params=pltpu.CompilerParams(
+            collective_id=1, has_side_effects=True, vmem_limit_bytes=VMEM_LIMIT
+        ),
+    )(field)
+
+
+def send_packed(packed):
+    flat = packed.reshape(packed.shape[0], -1, packed.shape[3])
+    got = lax.all_to_all(flat, ("gz", "gy"), split_axis=0, concat_axis=0, tiled=True)
+    return got.reshape(packed.shape)
 
 
 def small_dot(a, b):
@@ -410,10 +587,11 @@
     blocks = patch_force.shape[0]
     capacity = max(2, (2 * blocks + devices - 1) // devices)
 
-    packed = pack(patch_owner, patch_live, patch_force, patch_voxel, devices, capacity)
-    got = lax.all_to_all(
-        packed.reshape(devices, -1, packed.shape[3]), ("gz", "gy"), split_axis=0, concat_axis=0, tiled=True
-    ).reshape(packed.shape)
+    shares = (capacity // 2, capacity - capacity // 2)
+    near, far = pack(patch_owner, patch_live, patch_force, patch_voxel, devices, shares)
+    near = send_packed(near)
+    near, far = lax.optimization_barrier((near, far))
+    far = send_packed(far)
 
     weights = with_halo(voxel_mask, "gz", 0, 2, 1)
     weights = with_halo(weights, "gy", 1, 2, 1).astype(jnp.float32)
@@ -427,9 +605,9 @@
     inside_y = (node_y >= 0) & (node_y < groups_y * height)
     inside = (inside_z[:, None] & inside_y[None, :]).astype(jnp.float32)
 
-    force = scatter(got, capacity, depth, height, width).reshape(depth, height, ROWS, width)
-    field = with_halo(force, "gz", 0, 2, 2)
-    field = with_halo(field, "gy", 1, 2, 2)
+    force = scatter(near, shares[0], depth, height, width)
+    force = scatter(far, shares[1], depth, height, width, force)
+    field = field_with_halo(force.reshape(depth, height, ROWS, width), 2)
 
     applied, gram = first_operator(field, weights, matrix)
     norm_gram, curvature = total_grams(gram)

time: 329 us -> 249 us (0.76)
  blocking collectives: 99.2 us -> 0 us
  Pallas kernels: 78.2 us -> 155 us
  waiting for transfers between devices: 81 us -> 30 us
  starting transfers between devices: 37.3 us -> 28.1 us
  local copies, waits for them, and re-layouts: 17 us -> 21.9 us
    psum x2 -> x0, blocking collectives: 99.2 us -> none  [total_grams(): sums = lax.psum(jnp.sum(gram, axis=-1), ('gz', 'gy'))]
    pallas_call x2 -> x6, Pallas kernels: 34.4 us -> 111 us  [the longest x2 45.9 us: scatter(): pl.pallas_call(functools.partial(scatter_kernel, capacity), out_shape=jax...]
    all_to_all x1 -> x2, waiting for transfers between devices: 68.4 us -> 29.3 us  [send_packed(): lax.all_to_all(flat, ('gz', 'gy'), split_axis=0, concat_axis=0, tiled=True)]
    ppermute x4 -> x2, starting transfers between devices: 24.9 us -> 7.58 us  [with_halo(): lax.ppermute(lax.slice_in_dim(block, size - below, None, axis=dim), axis,...]
    all_to_all x1 -> x2, starting transfers between devices: 7.3 us -> 17.9 us  [send_packed(): lax.all_to_all(flat, ('gz', 'gy'), split_axis=0, concat_axis=0, tiled=True)]
    ppermute x4 -> x2, waiting for transfers between devices: 9.39 us -> 0.7 us  [with_halo(): lax.ppermute(lax.slice_in_dim(block, size - below, None, axis=dim), axis,...]
    unnamed x27 -> x35, local copies, waits for them, and re-layouts: 13.2 us -> 15.6 us
  transfers between devices with their start and end apart: 9 -> 6, of which waited for: 4 -> 3; matrix products, arithmetic and copies ran while one was open for 2% -> 2% of each run, Pallas kernels for 9% -> 14%
where the time goes in v2:
time: 249 us; the launch traced here: 248 us
  Pallas kernels  155 us (62%)
  waiting for transfers between devices  30 us (12%)
  starting transfers between devices  28.1 us (11%)
  local copies, waits for them, and re-layouts  21.9 us (9%)
  other arithmetic  10.3 us (4%)
    pallas_call x2, Pallas kernels, scatter(): pl.pallas_call(functools.partial(scatter_kernel, capacity), out_shape=jax...  45.9 us
    pallas_call x2, Pallas kernels, total_grams(): pl.pallas_call(functools.partial(reduce_kernel, (nz, ny)), out_shape=jax....  35.5 us
    all_to_all x2, waiting for transfers between devices, send_packed(): lax.all_to_all(flat, ('gz', 'gy'), split_axis=0, concat_axis=0, tiled=True)  29.3 us
    pallas_call x1, Pallas kernels, field_with_halo(): pl.pallas_call(functools.partial(halo_kernel, counts, halo), out_shape=ja...  24.3 us
    all_to_all x2, starting transfers between devices, send_packed(): lax.all_to_all(flat, ('gz', 'gy'), split_axis=0, concat_axis=0, tiled=True)  17.9 us
    pallas_call x1, Pallas kernels, first_operator(): pl.pallas_call(first_kernel, out_shape=(jax.ShapeDtypeStruct((depth - 1,...  17.6 us
    pallas_call x1, Pallas kernels, second_operator(): pl.pallas_call(second_kernel, out_shape=(jax.ShapeDtypeStruct((depth - 2,...  16.2 us
    unnamed x35, local copies, waits for them, and re-layouts  15.6 us
  transfers between devices with their start and end apart: 6, of which 3 were waited for; matrix products, arithmetic and copies ran while one was open for 2% of the time, Pallas kernels for 14%

profile of v2, /device:TPU:0, one launch (start us, length us, event | category | flops | bytes accessed | tf_op | source)
XLA Modules:
  0.0 247.5 jit_solution(16626102950341367718)
XLA Ops:
  0.6 0.8 copy.70.live_ref
  1.4 1.4 copy-done.6
  2.8 0.8 copy-done.7
  3.7 0.7 copy-done.10
  4.3 5.5 %shard_map.86 = (f32[32,13,8,128]{3,2,1,0:T(8,128)S(1)}, f32[32,13,8,128]{3,2,1,0:T(8,128)S(1)}) custom-call(s32[128]{0:T(128)S(1)} %copy-done.10, s32[128,8]{1,0:T(8,128)S(1)} %copy.70.live_ref, f32[128,24,128]{2,1,0:T(8,128)S(1)} %copy-done.6, s32[128,128]{1,0:T(8,128)S(1)} %copy-done.7), custom_call_target="tpu_custom_call" | custom-call | tf_op jit(solution)/shard_map/pallas_call | solution.py:88
  9.9 1.2 copy-done.2
  11.0 1.2 copy-done.3
  12.3 7.3 %all-to-all-start = ((f32[32,104,128]{2,1,0:T(8,128)}), f32[32,104,128]{2,1,0:T(8,128)S(1)}, u32[]{:S(2)}, u32[]{:S(2)}) async-start(f32[32,104,128]{2,1,0:T(8,128)} %bitcast.79), calls=%async_computation | async-start | bytes 3407872 | tf_op jit(solution)/shard_map/all_to_all | solution.py:574
  19.6 1.3 collective-permute-start.1
  20.9 4.5 %collective-permute-start = (s32[2,8,256]{2,1,0:T(8,128)S(1)}, s32[2,8,256]{2,1,0:T(8,128)S(1)}, u32[]{:S(2)}, u32[]{:S(2)}) collective-permute-start(s32[2,8,256]{2,1,0:T(8,128)S(1)} %slice.54), channel_id=1, source_target_pairs={{0,4},{4,8},{8,12},{12,16},{16,20},{20,24},{24,28},{1,5},{5,9},{9,... | collective-permute-start | bytes 49160 | tf_op jit(solution)/shard_map/ppermute | solution.py:411
  25.5 1.6 broadcast_multiply_fusion
  27.1 2.3 mul.140
  29.6 1.3 collective-permute-start.3
  30.9 3.0 %collective-permute-start.2 = (s32[11,2,256]{2,1,0:T(2,128)S(1)}, s32[11,2,256]{2,1,0:T(2,128)S(1)}, u32[]{:S(2)}, u32[]{:S(2)}) collective-permute-start(s32[11,2,256]{2,1,0:T(2,128)S(1)} %slice.65), channel_id=1, source_target_pairs={{0,1},{1,2},{2,3},{4,5},{5,6},{6,7},{8,9},{9,10},{10,11},{12,13},{... | collective-permute-start | bytes 67592 | tf_op jit(solution)/shard_map/ppermute | solution.py:411
  34.1 0.7 collective-permute-done.2
  34.9 25.2 %all-to-all-done = f32[32,104,128]{2,1,0:T(8,128)S(1)} async-done(((f32[32,104,128]{2,1,0:T(8,128)}), f32[32,104,128]{2,1,0:T(8,128)S(1)}, u32[]{:S(2)}, u32[]{:S(2)}) %all-to-all-start) | async-done | bytes 1703968 | tf_op jit(solution)/shard_map/all_to_all | solution.py:574
  60.1 10.6 %all-to-all-start.1 = ((f32[32,104,128]{2,1,0:T(8,128)}), f32[32,104,128]{2,1,0:T(8,128)}, u32[]{:S(2)}, u32[]{:S(2)}) async-start(f32[32,104,128]{2,1,0:T(8,128)} %bitcast.78), calls=%async_computation.1 | async-start | bytes 3407872 | tf_op jit(solution)/shard_map/all_to_all | solution.py:574
  71.1 34.8 %shard_map.87.refs_0_ = f32[64,24,256]{2,1,0:T(8,128)S(1)} custom-call(s32[128]{0:T(128)S(1)} %reshape.113.valid_ref, f32[32,13,8,128]{3,2,1,0:T(8,128)S(1)} %bitcast.77), custom_call_target="tpu_custom_call" | custom-call | flops 51539607552 | bytes 1703936 | tf_op jit(solution)/shard_map/pallas_call | solution.py:179
  105.9 1.1 copy-done.11
  107.0 4.1 %all-to-all-done.1 = f32[32,104,128]{2,1,0:T(8,128)} async-done(((f32[32,104,128]{2,1,0:T(8,128)}), f32[32,104,128]{2,1,0:T(8,128)}, u32[]{:S(2)}, u32[]{:S(2)}) %all-to-all-start.1) | async-done | bytes 1703968 | tf_op jit(solution)/shard_map/all_to_all | solution.py:574
  111.1 0.9 slice.64
  112.4 1.4 copy-done.12
  113.8 11.0 %shard_map.88 = f32[64,24,256]{2,1,0:T(8,128)S(1)} custom-call(s32[128]{0:T(128)S(1)} %reshape.111.valid_ref, f32[32,13,8,128]{3,2,1,0:T(8,128)} %bitcast.3.got_ref, f32[64,24,256]{2,1,0:T(8,128)S(1)} %copy-done.12), custom_call_target="tpu_custom_call" | custom-call | flops 51539607552 | bytes 1703936 | tf_op jit(solution)/shard_map/pallas_call | solution.py:179
  124.8 24.3 %shard_map.89.field_ref = f32[12,12,24,256]{3,2,1,0:T(8,128)S(1)} custom-call(f32[8,8,24,256]{3,2,1,0:T(8,128)S(1)} %bitcast.80), custom_call_target="tpu_custom_call" | custom-call | tf_op jit(solution)/shard_map/pallas_call | solution.py:558
  149.1 1.7 copy-done
  150.8 17.6 %shard_map.90 = (f32[11,10,24,256]{3,2,1,0:T(8,128)S(1)}, f32[8,128]{1,0:T(8,128)S(1)}) custom-call(f32[12,12,24,256]{3,2,1,0:T(8,128)} %copy-done, f32[11,11,256]{2,1,0:T(8,128)S(1)} %add_convert_fusion.weight_ref, bf16[192,576]{1,0:T(8,128)(2,1)S(1)} %pad_maximum_fusion.matrix_ref), custom_call_target="tpu_custom_call" | custom-call | tf_op jit(solution)/shard_map/pallas_call | solution.py:357
  168.5 1.5 copy-done.1
  170.0 0.6 copy-done.9
  170.6 24.9 %shard_map.91 = f32[8,128]{1,0:T(8,128)} custom-call(f32[8,128]{1,0:T(8,128)} %copy-done.9), custom_call_target="tpu_custom_call" | custom-call | tf_op jit(solution)/shard_map/pallas_call | solution.py:462
  195.5 0.7 slice_bitcast_fusion.1
  196.6 0.7 cholesky.59
  197.3 0.6 compare_reduce_fusion.2
  198.0 0.6 fusion.1
  198.6 0.6 custom-call.13
  199.7 0.7 cholesky.70
  200.4 0.6 compare_reduce_fusion.1
  201.1 0.6 fusion.2
  201.8 0.6 custom-call.15
  202.4 16.2 %shard_map.92 = (f32[8,8,24,256]{3,2,1,0:T(8,128)S(1)}, f32[9,8,24,256]{3,2,1,0:T(8,128)S(1)}, f32[8,128]{1,0:T(8,128)S(1)}) custom-call(f32[10,10]{1,0:T(8,128)S(1)} %and_convert_fusion.inside_ref, f32[1,8,8,256]{3,2,1,0:T(8,128)S(1)} %broadcast_in_dim.8.coef_ref, f32[12,12,24,256]{3,2,1,0:T(8,128)} %copy-done, f32[11,10,24,256]{3,2,1,0:T(8,128)} %copy-done.1, ...), custom_call_target="tpu_custom_call" | custom-call | tf_op jit(solution)/shard_map/pallas_call | solution.py:376
  218.7 1.1 copy-done.4
  220.4 10.6 %shard_map.93 = f32[8,128]{1,0:T(8,128)} custom-call(f32[8,128]{1,0:T(8,128)} %copy-done.8), custom_call_target="tpu_custom_call" | custom-call | tf_op jit(solution)/shard_map/pallas_call | solution.py:462
  231.0 0.7 slice_bitcast_fusion
  232.7 0.7 cholesky.81
  233.4 0.6 compare_reduce_fusion
  234.1 0.6 fusion.3
  234.7 0.6 custom-call.17
  236.0 1.4 copy-done.5
  237.4 10.2 %shard_map.94 = (f32[24,8,8,256]{3,2,1,0:T(8,128)}, f32[24,8,8,256]{3,2,1,0:T(8,128)}) custom-call(f32[3,8,8,256]{3,2,1,0:T(8,128)S(1)} %broadcast_in_dim.10.coef_ref, f32[12,12,24,256]{3,2,1,0:T(8,128)} %copy-done, f32[8,8,24,256]{3,2,1,0:T(8,128)S(1)} %copy-done.5, f32[11,10,24,256]{3,2,1,0:T(8,128)} %copy-done.1, ...), custom_call_target="tpu_custom_call" | custom-call | tf_op jit(solution)/shard_map/pallas_call | solution.py:397
  (83 shorter events, 4.2 us)
Async XLA Ops:
  1.4 1.4 copy-start.6
  2.8 0.8 copy-start.7
  3.7 0.7 copy-start.10
  9.9 1.2 copy-start.2
  11.0 1.2 copy-start.3
  12.3 7.3 %copy-start.14 = (s32[8,8,256]{2,1,0:T(8,128)S(1)}, s32[8,8,256]{2,1,0:T(8,128)}, u32[]{:S(2)}) copy-start(s32[8,8,256]{2,1,0:T(8,128)} %param.16) | copy-start | bytes 196612
  12.3 13.2 %copy-start.15 = (f32[24,24]{1,0:T(8,128)S(1)}, f32[24,24]{1,0:T(8,128)}, u32[]{:S(2)}) copy-start(f32[24,24]{1,0:T(8,128)} %param.17) | copy-start | bytes 6916
  12.3 47.8 %all-to-all-start = ((f32[32,104,128]{2,1,0:T(8,128)}), f32[32,104,128]{2,1,0:T(8,128)S(1)}, u32[]{:S(2)}, u32[]{:S(2)}) async-start(f32[32,104,128]{2,1,0:T(8,128)} %bitcast.79), calls=%async_computation | async-start | bytes 3407872 | tf_op jit(solution)/shard_map/all_to_all | solution.py:574
  19.6 10.0 %collective-permute-start.1 = (s32[1,8,256]{2,1,0:T(8,128)S(1)}, s32[1,8,256]{2,1,0:T(8,128)S(1)}, u32[]{:S(2)}, u32[]{:S(2)}) collective-permute-start(s32[1,8,256]{2,1,0:T(8,128)S(1)} %slice.55), channel_id=1, source_target_pairs={{4,0},{8,4},{12,8},{16,12},{20,16},{24,20},{28,24},{5,1},{9,5},{13... | collective-permute-start | bytes 24584 | tf_op jit(solution)/shard_map/ppermute | solution.py:412
  20.9 8.7 %collective-permute-start = (s32[2,8,256]{2,1,0:T(8,128)S(1)}, s32[2,8,256]{2,1,0:T(8,128)S(1)}, u32[]{:S(2)}, u32[]{:S(2)}) collective-permute-start(s32[2,8,256]{2,1,0:T(8,128)S(1)} %slice.54), channel_id=1, source_target_pairs={{0,4},{4,8},{8,12},{12,16},{16,20},{20,24},{24,28},{1,5},{5,9},{9,... | collective-permute-start | bytes 49160 | tf_op jit(solution)/shard_map/ppermute | solution.py:411
  29.6 4.5 %collective-permute-start.3 = (s32[11,1,256]{2,1,0:T(1,128)S(1)}, s32[11,1,256]{2,1,0:T(1,128)S(1)}, u32[]{:S(2)}, u32[]{:S(2)}) collective-permute-start(s32[11,1,256]{2,1,0:T(1,128)S(1)} %slice.66), channel_id=1, source_target_pairs={{1,0},{2,1},{3,2},{5,4},{6,5},{7,6},{9,8},{10,9},{11,10},{13,12},{... | collective-permute-start | bytes 33800 | tf_op jit(solution)/shard_map/ppermute | solution.py:412
  30.9 3.9 %collective-permute-start.2 = (s32[11,2,256]{2,1,0:T(2,128)S(1)}, s32[11,2,256]{2,1,0:T(2,128)S(1)}, u32[]{:S(2)}, u32[]{:S(2)}) collective-permute-start(s32[11,2,256]{2,1,0:T(2,128)S(1)} %slice.65), channel_id=1, source_target_pairs={{0,1},{1,2},{2,3},{4,5},{5,6},{6,7},{8,9},{9,10},{10,11},{12,13},{... | collective-permute-start | bytes 67592 | tf_op jit(solution)/shard_map/ppermute | solution.py:411
  60.1 51.0 %all-to-all-start.1 = ((f32[32,104,128]{2,1,0:T(8,128)}), f32[32,104,128]{2,1,0:T(8,128)}, u32[]{:S(2)}, u32[]{:S(2)}) async-start(f32[32,104,128]{2,1,0:T(8,128)} %bitcast.78), calls=%async_computation.1 | async-start | bytes 3407872 | tf_op jit(solution)/shard_map/all_to_all | solution.py:574
  105.9 1.1 copy-start.11
  112.4 1.4 copy-start.12
  149.1 1.8 copy-start
  150.8 45.6 %copy-start.13 = (f32[8,8,8]{2,1,0:T(8,128)S(1)}, f32[8,8,8]{2,1,0:T(8,128)}, u32[]{:S(2)}) copy-start(f32[8,8,8]{2,1,0:T(8,128)} %constant.59.clone) | copy-start | bytes 6148
  168.5 1.5 copy-start.1
  170.0 0.6 copy-start.9
  218.6 1.1 copy-start.4
  219.8 0.6 copy-start.8
  236.0 1.4 copy-start.5

commit v3 on v1

--- a/solution.py
+++ b/solution.py
@@ -24,7 +24,7 @@
 
 
 def to_diagonals(matrix):
-    return jnp.sum(DIAGONALS * matrix[None], axis=1)
+    return jnp.sum(DIAGONALS * matrix[None], axis=2)
 
 
 def from_diagonals(diagonals):
@@ -36,16 +36,17 @@
     return jnp.broadcast_to(stacked[..., None], stacked.shape + (width,))
 
 
-def pack_kernel(capacity, owner_ref, live_ref, force_ref, voxel_ref, out_ref, count_ref):
-    devices, rows, _, width = out_ref.shape
+def pack_kernel(shares, owner_ref, live_ref, force_ref, voxel_ref, near_ref, far_ref, count_ref):
     blocks = owner_ref.shape[0]
+    devices, _, _, width = near_ref.shape
     empty = jnp.full((8, width), -1.0, jnp.float32)
     zero = jnp.zeros((8, width), jnp.float32)
 
     def clear(dev, carry):
         count_ref[dev] = 0
-        for row in range(rows):
-            out_ref[dev, row] = zero if row < 3 * capacity else empty
+        for out_ref, share in zip((near_ref, far_ref), shares):
+            for row in range(out_ref.shape[1]):
+                out_ref[dev, row] = zero if row < 3 * share else empty
         return carry
 
     lax.fori_loop(0, devices, clear, 0)
@@ -60,29 +61,46 @@
         for load in range(1, LOADS):
             limit = jnp.where(sub == load, live_ref[block, load], limit)
         keep = lane < limit
-        for k in range(3):
-            value = force_ref[block, k * 8 : k * 8 + 8, :]
-            out_ref[owner, rank * 3 + k] = jnp.where(keep, value, 0.0)
+        values = [
+            jnp.where(keep, force_ref[block, k * 8 : k * 8 + 8, :], 0.0) for k in range(3)
+        ]
         ids = voxel_ref[pl.ds(block, 1), :].astype(jnp.float32)
-        out_ref[owner, 3 * capacity + rank // 8, pl.ds(rank % 8, 1), :] = ids
+
+        def store(out_ref, share, slot):
+            for k in range(3):
+                out_ref[owner, slot * 3 + k] = values[k]
+            out_ref[owner, 3 * share + slot // 8, pl.ds(slot % 8, 1), :] = ids
+
+        @pl.when(rank < shares[0])
+        def _():
+            store(near_ref, shares[0], rank)
+
+        @pl.when(rank >= shares[0])
+        def _():
+            store(far_ref, shares[1], rank - shares[0])
+
         return carry
 
     lax.fori_loop(0, blocks, place, 0)
 
 
-def pack(owner, live, force, voxel, devices, capacity):
-    rows = 3 * capacity + -(-capacity // 8)
+def pack(owner, live, force, voxel, devices, shares):
     return pl.pallas_call(
-        functools.partial(pack_kernel, capacity),
-        out_shape=jax.ShapeDtypeStruct((devices, rows, 8, force.shape[2]), jnp.float32),
+        functools.partial(pack_kernel, shares),
+        out_shape=tuple(
+            jax.ShapeDtypeStruct((devices, 3 * c + -(-c // 8), 8, force.shape[2]), jnp.float32)
+            for c in shares
+        ),
         in_specs=[SMEM, SMEM, VMEM, VMEM],
-        out_specs=VMEM,
+        out_specs=(VMEM, VMEM),
         scratch_shapes=[pltpu.SMEM((devices,), jnp.int32)],
         compiler_params=PARAMS,
     )(owner, live, force, voxel)
 
 
-def scatter_kernel(capacity, width_x, valid_ref, got_ref, out_ref, left_ref, acc_ref, list_ref):
+def scatter_kernel(capacity, valid_ref, got_ref, *refs):
+    before_ref = refs[0] if len(refs) == 5 else None
+    out_ref, left_ref, acc_ref, list_ref = refs[-4:]
     devices, rows, _, width = got_ref.shape
     total = devices * capacity
     slots = GROUP * width
@@ -137,35 +155,42 @@
             )
             return inner
 
-        lax.fori_loop(0, tiles, tile, 0)
+        lax.fori_loop(0, tiles, tile, 0, unroll=True)
         return carry
 
     lax.fori_loop(0, (count + GROUP - 1) // GROUP, step, 0)
     for r in range(SPLIT):
         for t in range(tiles):
-            out_ref[r * tiles + t] = (
-                acc_ref[t, r * 48 : r * 48 + 24, :] + acc_ref[t, r * 48 + 24 : r * 48 + 48, :]
-            )
-
-
-def scatter(got, capacity, depth, height, width_x):
+            high = acc_ref[t, r * 48 : r * 48 + 24, :]
+            result = high + acc_ref[t, r * 48 + 24 : r * 48 + 48, :]
+            if before_ref is not None:
+                result = result + before_ref[r * tiles + t]
+            out_ref[r * tiles + t] = result
+
+
+def scatter(got, capacity, depth, height, width_x, before=None):
     volume = depth * height * width_x
     tiles = volume // SPLIT // width_x
     assert volume // SPLIT == 1024
     first = got[:, 3 * capacity :, :, 0].reshape(got.shape[0], -1)[:, :capacity]
     valid = (first >= 0.0).astype(jnp.int32).reshape(-1)
+    arrays = (valid, got) if before is None else (valid, got, before)
+    slots = got.shape[0] * capacity * got.shape[3]
     return pl.pallas_call(
-        functools.partial(scatter_kernel, capacity, width_x),
+        functools.partial(scatter_kernel, capacity),
         out_shape=jax.ShapeDtypeStruct((depth * height, ROWS, width_x), jnp.float32),
-        in_specs=[SMEM, VMEM],
+        in_specs=[SMEM] + [VMEM] * (len(arrays) - 1),
         out_specs=VMEM,
+        cost_estimate=pl.CostEstimate(
+            flops=4 * SPLIT * 48 * 1024 * slots, bytes_accessed=4 * got.size, transcendentals=0
+        ),
         scratch_shapes=[
             pltpu.VMEM((SPLIT * 48, GROUP * got.shape[3]), jnp.bfloat16),
             pltpu.VMEM((tiles, SPLIT * 48, width_x), jnp.float32),
             pltpu.SMEM((valid.shape[0] + 1,), jnp.int32),
         ],
         compiler_params=PARAMS,
-    )(valid, got)
+    )(*arrays)
 
 
 def shift_left(value):
@@ -179,15 +204,22 @@
     return jnp.where(lane == 0, 0.0, pltpu.roll(value, 1, 1))
 
 
-def mixed(value, coefficients):
-    parts = []
-    for k in range(3):
-        piece = value[k * 8 : k * 8 + 8]
-        total = piece * coefficients[0]
-        for s in range(1, 8):
-            total = total + pltpu.roll(piece, s, 0) * coefficients[s]
-        parts.append(total)
-    return jnp.concatenate(parts, axis=0)
+def mixed(*terms):
+    width = terms[0][1][0].shape[1]
+    columns = []
+    for h in range(0, terms[0][0].shape[1], width):
+        parts = []
+        for k in range(3):
+            total = None
+            for s in range(8):
+                product = None
+                for value, coefficients in terms:
+                    piece = value[k * 8 : k * 8 + 8, h : h + width] * coefficients[s]
+                    product = piece if product is None else product + piece
+                total = product if s == 0 else total + pltpu.roll(product, s, 0)
+            parts.append(total)
+        columns.append(jnp.concatenate(parts, axis=0))
+    return jnp.concatenate(columns, axis=1)
 
 
 def store_split(split_ref, z, y, value):
@@ -198,12 +230,12 @@
     split_ref[z, y, 48:96, :] = low
 
 
-def run_operator(split_ref, field, weight_ref, weight_at, matrix_ref, out_ref, carry_ref):
+def run_operator(split_ref, field, weight_ref, matrix_ref, out_ref, carry_ref):
     planes, lines = split_ref.shape[0] - 1, split_ref.shape[1] - 1
     matrix = matrix_ref[...]
 
     def plane(ze, carry):
-        weights = weight_ref[ze + weight_at]
+        weights = weight_ref[ze]
         before = None
         for ye in range(lines):
             corners = [split_ref.at[ze + a, ye + b] for a in (0, 1) for b in (0, 1)]
@@ -214,7 +246,7 @@
                 jnp.concatenate([high, high, low], axis=0),
                 preferred_element_type=jnp.float32,
             )
-            forces = forces * weights[ye + weight_at : ye + weight_at + 1, :]
+            forces = forces * weights[ye : ye + 1, :]
             if ye > 0:
                 n = ye - 1
                 lower = forces[0:48] + before[48:96] + carry_ref[n]
@@ -229,7 +261,7 @@
 
 
 def run_grams(first, second, depth, height, gram_ref):
-    width = gram_ref.shape[-1]
+    width = gram_ref.shape[1]
 
     def plane(z, carry):
         sums = list(carry)
@@ -247,8 +279,11 @@
         return tuple(sums)
 
     sums = lax.fori_loop(0, depth, plane, tuple(jnp.zeros((8, width), jnp.float32) for _ in range(16)))
+    lane = lax.broadcasted_iota(jnp.int32, (8, width), 1)
+    tile = jnp.zeros((8, width), jnp.float32)
     for s in range(16):
-        gram_ref[s // 8, s % 8] = sums[s]
+        tile = jnp.where(lane == s, jnp.sum(sums[s], axis=1, keepdims=True), tile)
+    gram_ref[...] = tile
 
 
 def first_kernel(field_ref, weight_ref, matrix_ref, out_ref, gram_ref, split_ref, carry_ref):
@@ -261,19 +296,19 @@
 
     lax.fori_loop(0, depth, split, 0)
     run_operator(
-        split_ref, lambda z, y: field_ref[z, y], weight_ref, 0, matrix_ref, out_ref, carry_ref
+        split_ref, lambda z, y: field_ref[z, y], weight_ref, matrix_ref, out_ref, carry_ref
     )
     run_grams(
-        lambda z, y: field_ref[z + 2, y + 2],
-        lambda z, y: out_ref[z + 2, y + 1],
-        depth - 4,
-        lines - 4,
+        lambda z, y: field_ref[z + 1, y + 1],
+        lambda z, y: out_ref[z + 1, y],
+        depth - 2,
+        lines - 2,
         gram_ref,
     )
 
 
 def second_kernel(
-    inside_ref, coef_ref, field_ref, applied_ref, weight_ref, matrix_ref,
+    coef_ref, field_ref, applied_ref, weight_ref, matrix_ref,
     res_ref, out_ref, gram_ref, split_ref, carry_ref, full_ref,
 ):
     depth, lines = full_ref.shape[0], full_ref.shape[1]
@@ -281,15 +316,14 @@
     def split(z, carry):
         coef = [coef_ref[0, s] for s in range(8)]
         for y in range(lines):
-            value = field_ref[z + 1, y + 1] - mixed(applied_ref[z + 1, y], coef)
-            value = value * inside_ref[z, y]
+            value = field_ref[z, y] - mixed((applied_ref[z, y], coef))
             full_ref[z, y] = value
             store_split(split_ref, z, y, value)
         return carry
 
     lax.fori_loop(0, depth, split, 0)
     run_operator(
-        split_ref, lambda z, y: full_ref[z, y], weight_ref, 1, matrix_ref, out_ref, carry_ref
+        split_ref, lambda z, y: full_ref[z, y], weight_ref, matrix_ref, out_ref, carry_ref
     )
     run_grams(
         lambda z, y: full_ref[z + 1, y + 1],
@@ -314,9 +348,10 @@
         coefs = [[coef_ref[i, s] for s in range(8)] for i in range(3)]
         for y in range(lines):
             residual = res_ref[z, y]
-            disp = mixed(field_ref[z + 2, y + 2], coefs[0]) + mixed(residual, coefs[1])
-            left = residual - mixed(second_ref[z + 1, y], coefs[1])
-            left = left - mixed(first_ref[z + 2, y + 1], coefs[2])
+            disp = mixed((field_ref[z + 1, y + 1], coefs[0]), (residual, coefs[1]))
+            left = residual - mixed(
+                (second_ref[z + 1, y], coefs[1]), (first_ref[z + 1, y], coefs[2])
+            )
             disp_ref[:, z, y, :] = disp
             out_ref[:, z, y, :] = left
         return carry
@@ -330,7 +365,7 @@
         first_kernel,
         out_shape=(
             jax.ShapeDtypeStruct((depth - 1, lines - 2, ROWS, width), jnp.float32),
-            jax.ShapeDtypeStruct((2, 8, 8, 128), jnp.float32),
+            jax.ShapeDtypeStruct((8, 128), jnp.float32),
         ),
         in_specs=[VMEM] * 3,
         out_specs=(VMEM, VMEM),
@@ -342,17 +377,16 @@
     )(field, weights, matrix)
 
 
-def second_operator(inside, coef, field, applied, weights, matrix):
+def second_operator(coef, field, applied, weights, matrix):
     depth, lines, _, width = field.shape
-    depth, lines = depth - 2, lines - 2
     return pl.pallas_call(
         second_kernel,
         out_shape=(
             jax.ShapeDtypeStruct((depth - 2, lines - 2, ROWS, width), jnp.float32),
             jax.ShapeDtypeStruct((depth - 1, lines - 2, ROWS, width), jnp.float32),
-            jax.ShapeDtypeStruct((2, 8, 8, 128), jnp.float32),
+            jax.ShapeDtypeStruct((8, 128), jnp.float32),
         ),
-        in_specs=[SMEM] + [VMEM] * 5,
+        in_specs=[VMEM] * 5,
         out_specs=(VMEM, VMEM, VMEM),
         scratch_shapes=[
             pltpu.VMEM((depth, lines, 96, width), jnp.bfloat16),
@@ -360,7 +394,7 @@
             pltpu.VMEM((depth, lines, ROWS, width), jnp.float32),
         ],
         compiler_params=PARAMS,
-    )(inside, coef, field, applied, weights, matrix)
+    )(coef, field, applied, weights, matrix)
 
 
 def last_update(coef, field, residual, first, second):
@@ -375,14 +409,12 @@
     )(coef, field, residual, first, second)
 
 
-def with_halo(block, axis, dim, below, above):
+def with_below(block, axis, dim, below):
     count = lax.axis_size(axis)
     forward = [(i, i + 1) for i in range(count - 1)]
-    backward = [(target, source) for source, target in forward]
     size = block.shape[dim]
     low = lax.ppermute(lax.slice_in_dim(block, size - below, None, axis=dim), axis, forward)
-    high = lax.ppermute(lax.slice_in_dim(block, 0, above, axis=dim), axis, backward)
-    return jnp.concatenate([low, block, high], axis=dim)
+    return jnp.concatenate([low, block], axis=dim)
 
 
 def solve_small(matrix, target):
@@ -393,9 +425,242 @@
     )
 
 
-def total_grams(gram):
-    sums = lax.psum(jnp.sum(gram, axis=-1), ("gz", "gy"))
-    return from_diagonals(sums[0]), from_diagonals(sums[1])
+HALO = 1
+MESH = pl.DeviceIdType.MESH
+WAYS = [(dz, dy) for dz in (-1, 0, 1) for dy in (-1, 0, 1) if (dz, dy) != (0, 0)]
+
+
+def exists(counts, dz, dy):
+    z, y = lax.axis_index("gz") + dz, lax.axis_index("gy") + dy
+    return (z >= 0) & (z < counts[0]) & (y >= 0) & (y < counts[1])
+
+
+def greet(counts, ways, peers):
+    gz, gy = lax.axis_index("gz"), lax.axis_index("gy")
+    barrier = pltpu.get_barrier_semaphore()
+    for peer in peers:
+        pl.semaphore_signal(barrier, inc=1, device_id=peer, device_id_type=MESH)
+    total = jnp.int32(len(peers))
+    for dz, dy in ways:
+        total = total + jnp.where(exists(counts, dz, dy), 1, 0)
+
+        @pl.when(exists(counts, dz, dy))
+        def _():
+            pl.semaphore_signal(barrier, inc=1, device_id=(gz + dz, gy + dy), device_id_type=MESH)
+
+    pl.semaphore_wait(barrier, total)
+
+
+class Halo:
+    def __init__(self, counts, field_ref, first, out_ref, send_sems, recv_sems):
+        self.counts, self.field, self.first, self.out = counts, field_ref, first, out_ref
+        self.sems = (send_sems, recv_sems)
+        self.depth, self.lines = field_ref.shape[0] - first, field_ref.shape[1]
+
+    def source(self, step, size, first):
+        low = first + {-1: 0, 0: 0, 1: size - HALO}[step]
+        return pl.ds(low, size if step == 0 else HALO)
+
+    def target(self, step, size):
+        low = {-1: HALO + size, 0: HALO, 1: 0}[step]
+        return pl.ds(low, size if step == 0 else HALO)
+
+    def copy(self, i, sign):
+        dz, dy = WAYS[i]
+        return pltpu.make_async_remote_copy(
+            src_ref=self.field.at[
+                self.source(dz, self.depth, self.first), self.source(dy, self.lines, 0)
+            ],
+            dst_ref=self.out.at[self.target(dz, self.depth), self.target(dy, self.lines)],
+            send_sem=self.sems[0].at[i],
+            recv_sem=self.sems[1].at[i],
+            device_id=(lax.axis_index("gz") + sign * dz, lax.axis_index("gy") + sign * dy),
+            device_id_type=MESH,
+        )
+
+    def start(self):
+        for i, (dz, dy) in enumerate(WAYS):
+
+            @pl.when(exists(self.counts, dz, dy))
+            def _():
+                self.copy(i, 1).start()
+
+    def fill(self):
+        def keep(z, carry):
+            for y in range(self.lines):
+                self.out[z + HALO, y + HALO] = self.field[z + self.first, y]
+            return carry
+
+        lax.fori_loop(0, self.depth, keep, 0)
+        zero = jnp.zeros(self.out.shape[2:], jnp.float32)
+        for dz, dy in WAYS:
+
+            @pl.when(jnp.logical_not(exists(self.counts, -dz, -dy)))
+            def _():
+                zs, ys = self.target(dz, self.depth), self.target(dy, self.lines)
+
+                def clear(z, carry):
+                    for y in range(ys.size):
+                        self.out[zs.start + z, ys.start + y] = zero
+                    return carry
+
+                lax.fori_loop(0, zs.size, clear, 0)
+
+    def finish(self):
+        for i, (dz, dy) in enumerate(WAYS):
+
+            @pl.when(exists(self.counts, dz, dy))
+            def _():
+                self.copy(i, 1).wait_send()
+
+            @pl.when(exists(self.counts, -dz, -dy))
+            def _():
+                self.copy(i, -1).wait_recv()
+
+
+def lines_of_peers(counts):
+    gz, gy = lax.axis_index("gz"), lax.axis_index("gy")
+    beside = [(gz, lax.rem(gy + d, counts[1])) for d in range(1, counts[1])]
+    along = [(lax.rem(gz + d, counts[0]), gy) for d in range(1, counts[0])]
+    return beside, along
+
+
+def exchange(source_ref, slots_ref, place, peers, first, send_sems, recv_sems, meanwhile=None):
+    copies = [
+        pltpu.make_async_remote_copy(
+            src_ref=source_ref,
+            dst_ref=slots_ref.at[place],
+            send_sem=send_sems.at[first + i],
+            recv_sem=recv_sems.at[first + i],
+            device_id=peer,
+            device_id_type=MESH,
+        )
+        for i, peer in enumerate(peers)
+    ]
+    for copy in copies:
+        copy.start()
+    slots_ref[place] = source_ref[...]
+    if meanwhile is not None:
+        meanwhile()
+    for copy in copies:
+        copy.wait()
+    total = slots_ref[0]
+    for i in range(1, slots_ref.shape[0]):
+        total = total + slots_ref[i]
+    return total
+
+
+def reduce_kernel(counts, tile_ref, out_ref, line_ref, plane_ref, mid_ref, send_sems, recv_sems):
+    beside, along = lines_of_peers(counts)
+    greet(counts, [], beside + along)
+    sems = (send_sems, recv_sems)
+    mid_ref[...] = exchange(tile_ref, line_ref, lax.axis_index("gy"), beside, 0, *sems)
+    out_ref[...] = exchange(mid_ref, plane_ref, lax.axis_index("gz"), along, len(beside), *sems)
+
+
+def reduce_halo_kernel(
+    counts, tile_ref, field_ref, out_ref, full_ref,
+    line_ref, plane_ref, mid_ref, send_sems, recv_sems, halo_send, halo_recv,
+):
+    beside, along = lines_of_peers(counts)
+    greet(counts, [way for way in WAYS if 0 not in way], beside + along)
+    sems = (send_sems, recv_sems)
+    halo = Halo(counts, field_ref, 1, full_ref, halo_send, halo_recv)
+    mid_ref[...] = exchange(tile_ref, line_ref, lax.axis_index("gy"), beside, 0, *sems)
+
+    def meanwhile():
+        halo.start()
+        halo.fill()
+
+    out_ref[...] = exchange(
+        mid_ref, plane_ref, lax.axis_index("gz"), along, len(beside), *sems, meanwhile
+    )
+    halo.finish()
+
+
+def reduce_scratch(tile):
+    nz, ny = lax.axis_size("gz"), lax.axis_size("gy")
+    return [
+        pltpu.VMEM((ny,) + tile.shape, jnp.float32),
+        pltpu.VMEM((nz,) + tile.shape, jnp.float32),
+        pltpu.VMEM(tile.shape, jnp.float32),
+        pltpu.SemaphoreType.DMA((ny + nz - 2,)),
+        pltpu.SemaphoreType.DMA((ny + nz - 2,)),
+    ]
+
+
+HALO_SEMS = [pltpu.SemaphoreType.DMA((8,)), pltpu.SemaphoreType.DMA((8,))]
+
+
+def remote(number):
+    return pltpu.CompilerParams(
+        collective_id=number, has_side_effects=True, vmem_limit_bytes=VMEM_LIMIT
+    )
+
+
+def grams_of(tile):
+    sums = tile[:, :16].T
+    return from_diagonals(sums[:8]), from_diagonals(sums[8:])
+
+
+def total_grams(tile):
+    counts = (lax.axis_size("gz"), lax.axis_size("gy"))
+    sums = pl.pallas_call(
+        functools.partial(reduce_kernel, counts),
+        out_shape=jax.ShapeDtypeStruct(tile.shape, jnp.float32),
+        in_specs=[VMEM],
+        out_specs=VMEM,
+        scratch_shapes=reduce_scratch(tile),
+        compiler_params=remote(0),
+    )(tile)
+    return grams_of(sums)
+
+
+def padded_shape(depth, lines, rows, width):
+    return jax.ShapeDtypeStruct((depth + 2 * HALO, lines + 2 * HALO, rows, width), jnp.float32)
+
+
+def total_grams_with_halo(tile, field):
+    counts = (lax.axis_size("gz"), lax.axis_size("gy"))
+    depth, lines, rows, width = field.shape
+    sums, full = pl.pallas_call(
+        functools.partial(reduce_halo_kernel, counts),
+        out_shape=(
+            jax.ShapeDtypeStruct(tile.shape, jnp.float32),
+            padded_shape(depth - 1, lines, rows, width),
+        ),
+        in_specs=[VMEM, VMEM],
+        out_specs=(VMEM, VMEM),
+        scratch_shapes=reduce_scratch(tile) + HALO_SEMS,
+        compiler_params=remote(2),
+    )(tile, field)
+    return grams_of(sums) + (full,)
+
+
+def halo_kernel(counts, field_ref, out_ref, send_sems, recv_sems):
+    greet(counts, WAYS, [])
+    halo = Halo(counts, field_ref, 0, out_ref, send_sems, recv_sems)
+    halo.start()
+    halo.fill()
+    halo.finish()
+
+
+def field_with_halo(field):
+    counts = (lax.axis_size("gz"), lax.axis_size("gy"))
+    return pl.pallas_call(
+        functools.partial(halo_kernel, counts),
+        out_shape=padded_shape(*field.shape),
+        in_specs=[VMEM],
+        out_specs=VMEM,
+        scratch_shapes=HALO_SEMS,
+        compiler_params=remote(1),
+    )(field)
+
+
+def send_packed(packed):
+    flat = packed.reshape(packed.shape[0], -1, packed.shape[3])
+    got = lax.all_to_all(flat, ("gz", "gy"), split_axis=0, concat_axis=0, tiled=True)
+    return got.reshape(packed.shape)
 
 
 def small_dot(a, b):
@@ -410,34 +675,30 @@
     blocks = patch_force.shape[0]
     capacity = max(2, (2 * blocks + devices - 1) // devices)
 
-    packed = pack(patch_owner, patch_live, patch_force, patch_voxel, devices, capacity)
-    got = lax.all_to_all(
-        packed.reshape(devices, -1, packed.shape[3]), ("gz", "gy"), split_axis=0, concat_axis=0, tiled=True
-    ).reshape(packed.shape)
-
-    weights = with_halo(voxel_mask, "gz", 0, 2, 1)
-    weights = with_halo(weights, "gy", 1, 2, 1).astype(jnp.float32)
+    shares = (capacity // 2, capacity - capacity // 2)
+    near, far = pack(patch_owner, patch_live, patch_force, patch_voxel, devices, shares)
+    near = send_packed(near)
+    near, far = lax.optimization_barrier((near, far))
+    far = send_packed(far)
+
+    weights = with_below(voxel_mask, "gz", 0, 1)
+    weights = with_below(weights, "gy", 1, 1).astype(jnp.float32)
     wide = jnp.kron(element_matrix, jnp.eye(LOADS, dtype=jnp.float32))
     high = wide.astype(jnp.bfloat16)
     low = (wide - lax.reduce_precision(wide, 8, 7)).astype(jnp.bfloat16)
     matrix = jnp.concatenate([high, low, high], axis=1)
-    node_z = jnp.arange(depth + 2) - 1 + lax.axis_index("gz") * depth
-    node_y = jnp.arange(height + 2) - 1 + lax.axis_index("gy") * height
-    inside_z = (node_z >= 0) & (node_z < groups_z * depth)
-    inside_y = (node_y >= 0) & (node_y < groups_y * height)
-    inside = (inside_z[:, None] & inside_y[None, :]).astype(jnp.float32)
-
-    force = scatter(got, capacity, depth, height, width).reshape(depth, height, ROWS, width)
-    field = with_halo(force, "gz", 0, 2, 2)
-    field = with_halo(field, "gy", 1, 2, 2)
+
+    force = scatter(near, shares[0], depth, height, width)
+    force = scatter(far, shares[1], depth, height, width, force)
+    field = field_with_halo(force.reshape(depth, height, ROWS, width))
 
     applied, gram = first_operator(field, weights, matrix)
-    norm_gram, curvature = total_grams(gram)
+    norm_gram, curvature, around = total_grams_with_halo(gram, applied)
     curvature = 0.5 * (curvature + curvature.T)
     alpha = solve_small(curvature, norm_gram)
 
     residual, again, gram = second_operator(
-        inside, spread([alpha], width), field, applied, weights, matrix
+        spread([alpha], 128), field, around, weights, matrix
     )
     norm_next, cross = total_grams(gram)
     beta = solve_small(norm_gram, norm_next)
@@ -446,7 +707,7 @@
     alpha_next = solve_small(curvature, norm_next)
     joint = small_dot(beta, alpha_next)
 
-    coef = spread([alpha + joint, alpha_next, joint], width)
+    coef = spread([alpha + joint, alpha_next, joint], 128)
     return last_update(coef, field, residual, applied, again)
 
 

time: 329 us -> 216 us (0.66)
  blocking collectives: 99.2 us -> 0 us
  Pallas kernels: 78.2 us -> 112 us
  waiting for transfers between devices: 81 us -> 49.6 us
  starting transfers between devices: 37.3 us -> 20.9 us
    psum x2 -> x0, blocking collectives: 99.2 us -> none  [total_grams(): sums = lax.psum(jnp.sum(gram, axis=-1), ('gz', 'gy'))]
    pallas_call x2 -> x6, Pallas kernels: 34.4 us -> 76.2 us  [the longest x2 25 us: scatter(): pl.pallas_call(functools.partial(scatter_kernel, capacity), out_shape=jax...]
    ppermute x8 -> x2, starting transfers between devices: 30 us -> 5.15 us  [with_below(): lax.ppermute(lax.slice_in_dim(block, size - below, None, axis=dim), axis,...]
    all_to_all x1 -> x2, waiting for transfers between devices: 68.4 us -> 48.2 us  [send_packed(): lax.all_to_all(flat, ('gz', 'gy'), split_axis=0, concat_axis=0, tiled=True)]
    ppermute x8 -> x2, waiting for transfers between devices: 12.5 us -> 1.37 us  [with_below(): lax.ppermute(lax.slice_in_dim(block, size - below, None, axis=dim), axis,...]
    all_to_all x1 -> x2, starting transfers between devices: 7.3 us -> 15.7 us  [send_packed(): lax.all_to_all(flat, ('gz', 'gy'), split_axis=0, concat_axis=0, tiled=True)]
    pallas_call x1, Pallas kernels: 17.5 us -> 11.7 us  [first_operator(): pl.pallas_call(first_kernel, out_shape=(jax.ShapeDtypeStruct((depth - 1,...]
    unnamed x27 -> x38, local copies, waits for them, and re-layouts: 13.2 us -> 15.3 us
  transfers between devices with their start and end apart: 9 -> 4, of which waited for: 4 -> 4; matrix products, arithmetic and copies ran while one was open for 2% -> 2% of each run, Pallas kernels for 9% -> 9%
where the time goes in v3:
time: 216 us; the launch traced here: 215 us
  Pallas kernels  112 us (52%)
  waiting for transfers between devices  49.6 us (23%)
  starting transfers between devices  20.9 us (10%)
  local copies, waits for them, and re-layouts  20.2 us (9%)
  other arithmetic  10.4 us (5%)
    all_to_all x2, waiting for transfers between devices, send_packed(): lax.all_to_all(flat, ('gz', 'gy'), split_axis=0, concat_axis=0, tiled=True)  48.2 us
    pallas_call x2, Pallas kernels, scatter(): pl.pallas_call(functools.partial(scatter_kernel, capacity), out_shape=jax...  25 us
    pallas_call x1, Pallas kernels, total_grams_with_halo(): pl.pallas_call(functools.partial(reduce_halo_kernel, counts), out_shape=(...  23 us
    pallas_call x1, Pallas kernels, second_operator(): pl.pallas_call(second_kernel, out_shape=(jax.ShapeDtypeStruct((depth - 2,...  15.8 us
    all_to_all x2, starting transfers between devices, send_packed(): lax.all_to_all(flat, ('gz', 'gy'), split_axis=0, concat_axis=0, tiled=True)  15.7 us
    unnamed x38, local copies, waits for them, and re-layouts  15.3 us
    pallas_call x1, Pallas kernels, field_with_halo(): pl.pallas_call(functools.partial(halo_kernel, counts), out_shape=padded_s...  14.2 us
    pallas_call x1, Pallas kernels, first_operator(): pl.pallas_call(first_kernel, out_shape=(jax.ShapeDtypeStruct((depth - 1,...  11.7 us
  transfers between devices with their start and end apart: 4, of which 4 were waited for; matrix products, arithmetic and copies ran while one was open for 2% of the time, Pallas kernels for 9%

profile of v3, /device:TPU:0, one launch (start us, length us, event | category | flops | bytes accessed | tf_op | source)
XLA Modules:
  0.0 214.8 jit_solution(13360111590247891738)
XLA Ops:
  0.6 0.8 copy.70.live_ref
  1.4 1.4 copy-done.8
  2.8 0.8 copy-done.11
  3.7 0.7 copy-done.12
  4.3 5.5 %shard_map.86 = (f32[32,13,8,128]{3,2,1,0:T(8,128)S(1)}, f32[32,13,8,128]{3,2,1,0:T(8,128)S(1)}) custom-call(s32[128]{0:T(128)S(1)} %copy-done.12, s32[128,8]{1,0:T(8,128)S(1)} %copy.70.live_ref, f32[128,24,128]{2,1,0:T(8,128)S(1)} %copy-done.8, s32[128,128]{1,0:T(8,128)S(1)} %copy-done.11), custom_call_target="tpu_custom_call" | custom-call | tf_op jit(solution)/shard_map/pallas_call | solution.py:88
  9.9 1.2 copy-done.6
  11.0 1.2 copy-done.7
  12.3 7.3 %all-to-all-start = ((f32[32,104,128]{2,1,0:T(8,128)}), f32[32,104,128]{2,1,0:T(8,128)S(1)}, u32[]{:S(2)}, u32[]{:S(2)}) async-start(f32[32,104,128]{2,1,0:T(8,128)} %bitcast.79), calls=%async_computation | async-start | bytes 3407872 | tf_op jit(solution)/shard_map/all_to_all | solution.py:662
  19.6 3.7 %collective-permute-start = (s32[1,8,256]{2,1,0:T(8,128)S(1)}, s32[1,8,256]{2,1,0:T(8,128)S(1)}, u32[]{:S(2)}, u32[]{:S(2)}) collective-permute-start(s32[1,8,256]{2,1,0:T(8,128)S(1)} %slice.48), channel_id=1, source_target_pairs={{0,4},{4,8},{8,12},{12,16},{16,20},{20,24},{24,28},{1,5},{5,9},{9,... | collective-permute-start | bytes 24584 | tf_op jit(solution)/shard_map/ppermute | solution.py:416
  23.3 1.6 broadcast_multiply_fusion
  24.9 2.3 %mul.134 = f32[192,192]{1,0:T(8,128)S(1)} reshape(f32[24,8,24,8]{3,2,1,0:T(8,128)} %broadcast_multiply_fusion) | data formatting | bytes 294912 | tf_op jit(solution)/shard_map/jit(kron)/mul | solution.py:686
  27.3 0.7 collective-permute-done
  28.0 1.5 collective-permute-start.1
  29.6 0.7 collective-permute-done.1
  30.3 29.7 %all-to-all-done = f32[32,104,128]{2,1,0:T(8,128)S(1)} async-done(((f32[32,104,128]{2,1,0:T(8,128)}), f32[32,104,128]{2,1,0:T(8,128)S(1)}, u32[]{:S(2)}, u32[]{:S(2)}) %all-to-all-start) | async-done | bytes 1703968 | tf_op jit(solution)/shard_map/all_to_all | solution.py:662
  60.0 8.4 %all-to-all-start.1 = ((f32[32,104,128]{2,1,0:T(8,128)}), f32[32,104,128]{2,1,0:T(8,128)}, u32[]{:S(2)}, u32[]{:S(2)}) async-start(f32[32,104,128]{2,1,0:T(8,128)} %bitcast.78), calls=%async_computation.1 | async-start | bytes 3407872 | tf_op jit(solution)/shard_map/all_to_all | solution.py:662
  68.8 20.4 %shard_map.87.refs_0_ = f32[64,24,256]{2,1,0:T(8,128)S(1)} custom-call(s32[128]{0:T(128)S(1)} %reshape.97.valid_ref, f32[32,13,8,128]{3,2,1,0:T(8,128)S(1)} %bitcast.77), custom_call_target="tpu_custom_call" | custom-call | flops 51539607552 | bytes 1703936 | tf_op jit(solution)/shard_map/pallas_call | solution.py:179
  89.1 1.1 copy-done.13
  90.3 18.5 %all-to-all-done.1 = f32[32,104,128]{2,1,0:T(8,128)} async-done(((f32[32,104,128]{2,1,0:T(8,128)}), f32[32,104,128]{2,1,0:T(8,128)}, u32[]{:S(2)}, u32[]{:S(2)}) %all-to-all-start.1) | async-done | bytes 1703968 | tf_op jit(solution)/shard_map/all_to_all | solution.py:662
  108.8 0.9 slice.56
  110.1 1.4 copy-done.14
  111.5 4.6 %shard_map.88 = f32[64,24,256]{2,1,0:T(8,128)S(1)} custom-call(s32[128]{0:T(128)S(1)} %reshape.95.valid_ref, f32[32,13,8,128]{3,2,1,0:T(8,128)} %bitcast.3.got_ref, f32[64,24,256]{2,1,0:T(8,128)S(1)} %copy-done.14), custom_call_target="tpu_custom_call" | custom-call | flops 51539607552 | bytes 1703936 | tf_op jit(solution)/shard_map/pallas_call | solution.py:179
  116.1 14.2 %shard_map.89.field_ref = f32[10,10,24,256]{3,2,1,0:T(8,128)S(1)} custom-call(f32[8,8,24,256]{3,2,1,0:T(8,128)S(1)} %bitcast.80), custom_call_target="tpu_custom_call" | custom-call | tf_op jit(solution)/shard_map/pallas_call | solution.py:650
  130.3 11.7 %shard_map.90 = (f32[9,8,24,256]{3,2,1,0:T(8,128)S(1)}, f32[8,128]{1,0:T(8,128)S(1)}) custom-call(f32[10,10,24,256]{3,2,1,0:T(8,128)S(1)} %shard_map.89.field_ref, f32[9,9,256]{2,1,0:T(8,128)S(1)} %add_convert_fusion.weight_ref, bf16[192,576]{1,0:T(8,128)(2,1)S(1)} %pad_maximum_fusion.matrix_ref), custom_call_target="tpu_custom_call" | custom-call | tf_op jit(solution)/shard_map/pallas_call | solution.py:364
  142.0 23.0 %shard_map.91 = (f32[8,128]{1,0:T(8,128)S(1)}, f32[10,10,24,256]{3,2,1,0:T(8,128)S(1)}) custom-call(f32[8,128]{1,0:T(8,128)S(1)} %get-tuple-element.20.tile_ref, f32[9,8,24,256]{3,2,1,0:T(8,128)S(1)} %get-tuple-element.21.field_ref.first_ref), custom_call_target="tpu_custom_call" | custom-call | tf_op jit(solution)/shard_map/pallas_call | solution.py:626
  165.0 1.4 copy-done.3
  166.8 0.7 cholesky.59
  167.6 0.6 compare_reduce_fusion.2
  168.2 0.6 fusion.1
  168.9 0.6 custom-call.13
  169.6 0.2 fusion.12
  170.0 0.7 cholesky.70
  170.8 0.6 compare_reduce_fusion.1
  171.4 0.6 fusion.2
  172.1 0.6 custom-call.15
  172.8 15.8 %shard_map.92 = (f32[8,8,24,256]{3,2,1,0:T(8,128)S(1)}, f32[9,8,24,256]{3,2,1,0:T(8,128)S(1)}, f32[8,128]{1,0:T(8,128)S(1)}) custom-call(f32[1,8,8,128]{3,2,1,0:T(8,128)S(1)} %broadcast_in_dim.9.coef_ref, f32[10,10,24,256]{3,2,1,0:T(8,128)} %copy-done, f32[10,10,24,256]{3,2,1,0:T(8,128)} %copy-done.3, f32[9,9,256]{2,1,0:T(8,128)S(1)} %add_convert_fusion.weight_ref, ...), custom_call_target="tpu_custom_call" | custom-call | tf_op jit(solution)/shard_map/pallas_call | solution.py:382
  188.5 1.2 copy-done.4
  189.7 1.1 copy-done.9
  190.9 8.5 %shard_map.93 = f32[8,128]{1,0:T(8,128)S(1)} custom-call(f32[8,128]{1,0:T(8,128)S(1)} %get-tuple-element.24.tile_ref), custom_call_target="tpu_custom_call" | custom-call | tf_op jit(solution)/shard_map/pallas_call | solution.py:608
  199.6 0.2 fusion.8
  200.4 0.7 cholesky.81
  201.1 0.6 compare_reduce_fusion
  201.8 0.6 fusion.3
  202.4 0.6 custom-call.17
  203.1 0.2 fusion.4
  203.7 1.5 copy-done.5
  205.2 1.4 copy-done.10
  206.6 8.2 %shard_map.94 = (f32[24,8,8,256]{3,2,1,0:T(8,128)}, f32[24,8,8,256]{3,2,1,0:T(8,128)}) custom-call(f32[3,8,8,128]{3,2,1,0:T(8,128)S(1)} %broadcast_in_dim.10.coef_ref, f32[10,10,24,256]{3,2,1,0:T(8,128)} %copy-done, f32[8,8,24,256]{3,2,1,0:T(8,128)S(1)} %copy-done.10, f32[9,8,24,256]{3,2,1,0:T(8,128)S(1)} %copy-done.2, f32[9,8,24,256]{3,2,1,0:T(8,128)S(1)} %copy-done.5), custom_call_target="tpu_custom_call" | custom-call | tf_op jit(solution)/shard_map/pallas_call | solution.py:403
  (78 shorter events, 3.0 us)
Async XLA Ops:
  1.4 1.4 copy-start.8
  2.8 0.8 copy-start.11
  3.7 0.7 copy-start.12
  9.9 1.2 copy-start.6
  11.0 1.2 copy-start.7
  12.3 7.3 %copy-start.16 = (s32[8,8,256]{2,1,0:T(8,128)S(1)}, s32[8,8,256]{2,1,0:T(8,128)}, u32[]{:S(2)}) copy-start(s32[8,8,256]{2,1,0:T(8,128)} %param.16) | copy-start | bytes 196612
  12.3 11.0 %copy-start.17 = (f32[24,24]{1,0:T(8,128)S(1)}, f32[24,24]{1,0:T(8,128)}, u32[]{:S(2)}) copy-start(f32[24,24]{1,0:T(8,128)} %param.17) | copy-start | bytes 6916
  12.3 47.7 %all-to-all-start = ((f32[32,104,128]{2,1,0:T(8,128)}), f32[32,104,128]{2,1,0:T(8,128)S(1)}, u32[]{:S(2)}, u32[]{:S(2)}) async-start(f32[32,104,128]{2,1,0:T(8,128)} %bitcast.79), calls=%async_computation | async-start | bytes 3407872 | tf_op jit(solution)/shard_map/all_to_all | solution.py:662
  19.6 8.4 %collective-permute-start = (s32[1,8,256]{2,1,0:T(8,128)S(1)}, s32[1,8,256]{2,1,0:T(8,128)S(1)}, u32[]{:S(2)}, u32[]{:S(2)}) collective-permute-start(s32[1,8,256]{2,1,0:T(8,128)S(1)} %slice.48), channel_id=1, source_target_pairs={{0,4},{4,8},{8,12},{12,16},{16,20},{20,24},{24,28},{1,5},{5,9},{9,... | collective-permute-start | bytes 24584 | tf_op jit(solution)/shard_map/ppermute | solution.py:416
  28.0 2.3 %collective-permute-start.1 = (s32[9,1,256]{2,1,0:T(1,128)S(1)}, s32[9,1,256]{2,1,0:T(1,128)S(1)}, u32[]{:S(2)}, u32[]{:S(2)}) collective-permute-start(s32[9,1,256]{2,1,0:T(1,128)S(1)} %slice.57), channel_id=1, source_target_pairs={{0,1},{1,2},{2,3},{4,5},{5,6},{6,7},{8,9},{9,10},{10,11},{12,13},{... | collective-permute-start | bytes 27656 | tf_op jit(solution)/shard_map/ppermute | solution.py:416
  60.0 48.8 %all-to-all-start.1 = ((f32[32,104,128]{2,1,0:T(8,128)}), f32[32,104,128]{2,1,0:T(8,128)}, u32[]{:S(2)}, u32[]{:S(2)}) async-start(f32[32,104,128]{2,1,0:T(8,128)} %bitcast.78), calls=%async_computation.1 | async-start | bytes 3407872 | tf_op jit(solution)/shard_map/all_to_all | solution.py:662
  89.1 1.1 copy-start.13
  110.1 1.4 copy-start.14
  130.3 34.7 %copy-start = (f32[10,10,24,256]{3,2,1,0:T(8,128)}, f32[10,10,24,256]{3,2,1,0:T(8,128)S(1)}, u32[]{:S(2)}) copy-start(f32[10,10,24,256]{3,2,1,0:T(8,128)S(1)} %shard_map.89.field_ref) | copy-start | bytes 7372804
  130.3 36.4 %copy-start.15 = (f32[8,8,8]{2,1,0:T(8,128)S(1)}, f32[8,8,8]{2,1,0:T(8,128)}, u32[]{:S(2)}) copy-start(f32[8,8,8]{2,1,0:T(8,128)} %constant.39.clone) | copy-start | bytes 6148
  142.0 24.5 %copy-start.1 = (f32[9,8,24,256]{3,2,1,0:T(8,128)}, f32[9,8,24,256]{3,2,1,0:T(8,128)S(1)}, u32[]{:S(2)}) copy-start(f32[9,8,24,256]{3,2,1,0:T(8,128)S(1)} %get-tuple-element.21.field_ref.first_ref) | copy-start | bytes 5308420
  165.0 1.4 copy-start.3
  172.8 31.0 %copy-start.2 = (f32[9,8,24,256]{3,2,1,0:T(8,128)S(1)}, f32[9,8,24,256]{3,2,1,0:T(8,128)}, u32[]{:S(2)}) copy-start(f32[9,8,24,256]{3,2,1,0:T(8,128)} %copy-done.1) | copy-start | bytes 5308420
  188.5 1.2 copy-start.4
  189.7 1.1 copy-start.9
  203.7 1.5 copy-start.5
  205.2 1.4 copy-start.10
